TPU v7x, 32 devices: a whole 2x2x4 slice. The times are simulated.
32 devices in a mesh: dp: 8 (over z, x), grp: 4 (over y, core).
Axes of the slice: x: 2, y: 2, z: 4, core: 2. Of those that a mesh axis runs over, the one named last changes fastest.
Arguments:
- doc_tokens: bfloat16 [32, 512, 768], P(('dp', 'grp')), may hold values from -6 to 6
- doc_lengths: int32 [32, 4], P(('dp', 'grp')), may hold values from 1 to 256, 480 in all within a row
- query_tokens: bfloat16 [64, 32, 768], P(('dp', 'grp')), may hold values from -6 to 6
- query_lengths: int32 [64], P(('dp', 'grp')), may hold values from 8 to 32
- candidates: int32 [64, 32], P(('dp', 'grp')), may hold values from 0 to 31
- labels: int32 [64], P(('dp', 'grp')), may hold values from 0 to 31
- gain_attn: bfloat16 [768], replicated, may hold values from 0.5 to 1.5
- w_query: bfloat16 [768, 768], replicated, may hold values from -0.02734375 to 0.02734375
- w_key: bfloat16 [768, 768], replicated, may hold values from -0.21875 to 0.21875
- w_value: bfloat16 [768, 768], replicated, may hold values from -0.21875 to 0.21875
- w_out: bfloat16 [768, 768], replicated, may hold values from -0.875 to 0.875
- bias_table: bfloat16 [32, 12], replicated, may hold values from -4 to 4
- gain_ffn: bfloat16 [768], replicated, may hold values from 0.5 to 1.5
- w_gate: bfloat16 [768, 2048], replicated, may hold values from -0.21875 to 0.21875
- w_up: bfloat16 [768, 2048], replicated, may hold values from -0.21875 to 0.21875
- w_down: bfloat16 [2048, 768], replicated, may hold values from -0.125 to 0.125
- gain_final: bfloat16 [768], replicated, may hold values from 0.5 to 1.5
- w_proj: bfloat16 [768, 128], replicated, may hold values from -0.21875 to 0.21875
Outputs:
- loss: float32 [], replicated
- doc_grad: float32 [32, 512, 768], P(('dp', 'grp'))
- query_grad: float32 [64, 32, 768], P(('dp', 'grp'))
- gain_attn_grad: float32 [768], P(('dp', 'grp'))
- w_query_grad: float32 [768, 768], P(('dp', 'grp'))
- w_key_grad: float32 [768, 768], P(('dp', 'grp'))
- w_value_grad: float32 [768, 768], P(('dp', 'grp'))
- w_out_grad: float32 [768, 768], P(('dp', 'grp'))
- bias_table_grad: float32 [32, 12], replicated
- gain_ffn_grad: float32 [768], P(('dp', 'grp'))
- w_gate_grad: float32 [768, 2048], P(('dp', 'grp'))
- w_up_grad: float32 [768, 2048], P(('dp', 'grp'))
- w_down_grad: float32 [2048, 768], P(('dp', 'grp'))
- gain_final_grad: float32 [768], P(('dp', 'grp'))
- w_proj_grad: float32 [768, 128], P(('dp', 'grp'))
Inputs may be any that keep to these rules, and one draw needn't show every extreme that they name: `doc_lengths`: the lengths of each row's 4 documents sum to 480, and in every row the longest is 256. `candidates`: numbers of blocks of the query's own group.
All inputs are finite; a program needn't handle non-finite values.
Results may differ from a plain program's by a relative error of at most 0.017.
Values may be sent and summed in bfloat16 or wider, within the bound.
No kernel may reach another device: no remote copies, remote signals or barrier semaphores. Data moves between devices by JAX's collectives and lax.ppermute only.
A program may use at most 192 MiB of HBM per device.

v0:
```python
import jax
import jax.numpy as jnp
import numpy as np
from jax import lax
from jax.sharding import PartitionSpec as P

BUCKETS = 32
DIST = 128
BLK = 128


eps_norm = 1e-06
normalizer_sharpness = 0.25
logit_scale = 16.0
excluded_entry_default = -1e30
highest = lax.Precision.HIGHEST


def bucket_index(length):
    positions = np.arange(length)
    offsets = positions[None, :] - positions[:, None]
    half_count = BUCKETS // 2
    exact_count = half_count // 2
    distance = np.abs(offsets)
    scaled = (
        np.log(np.maximum(distance, 1) / exact_count)
        / np.log(DIST / exact_count)
        * (half_count - exact_count)
    )
    far_bucket = np.minimum(exact_count + np.maximum(scaled, 0).astype(np.int64), half_count - 1)
    bucket = (offsets > 0) * half_count + np.where(distance < exact_count, distance, far_bucket)
    return bucket.astype(np.int32)


def bucket_blocks(length):
    step_rows = min(length, 128)
    return jnp.asarray(bucket_index(length)).reshape(length // step_rows, step_rows, length)


def bucket_onehot(index_block, bucket_total):
    return (
        index_block[:, :, None] == jnp.arange(bucket_total, dtype=jnp.int32)[None, None, :]
    ).astype(jnp.float32)


def relative_bias(bias_table, length):
    blocks = bucket_blocks(length)
    bucket_total, head_total = bias_table.shape

    def relative_one_block(index_block):
        return jnp.einsum(
            "qku,uh->hqk", bucket_onehot(index_block, bucket_total), bias_table, precision=highest
        )

    pieces = lax.map(relative_one_block, blocks)
    return jnp.transpose(pieces, (1, 0, 2, 3)).reshape(head_total, length, length)


def bias_gradient(dscore_sum, length, bucket_total):
    blocks = bucket_blocks(length)
    head_total = dscore_sum.shape[0]
    block_total, step_rows = (blocks.shape[0], blocks.shape[1])
    grad_blocks = jnp.transpose(
        dscore_sum.reshape(head_total, block_total, step_rows, length), (1, 0, 2, 3)
    )

    def bias_one_block(total, parts):
        index_block, grad_block = parts
        return (
            total
            + jnp.einsum(
                "hqk,qku->uh",
                grad_block,
                bucket_onehot(index_block, bucket_total),
                precision=highest,
            ),
            None,
        )

    total, _ = lax.scan(
        bias_one_block, jnp.zeros((bucket_total, head_total), jnp.float32), (blocks, grad_blocks)
    )
    return total


def rms_norm(values, gain_vec):
    return (
        values * lax.rsqrt(jnp.mean(values * values, axis=-1, keepdims=True) + eps_norm) * gain_vec
    )


def unit_scale(projected):
    return projected * lax.rsqrt(jnp.sum(projected * projected, axis=-1, keepdims=True) + eps_norm)


def gated_unit(gate_pre, upward):
    return jax.nn.gelu(gate_pre, approximate=True) * upward


def matmul(left, right):
    return jnp.dot(left, right, preferred_element_type=jnp.float32)


def matmul_tn(left, right):
    return lax.dot_general(
        left, right, (((0,), (0,)), ((), ())), preferred_element_type=jnp.float32
    )


def matmul_nt(left, right):
    return lax.dot_general(
        left, right, (((1,), (1,)), ((), ())), preferred_element_type=jnp.float32
    )


def document_mask(lengths_rows, length):
    doc_ends = jnp.cumsum(lengths_rows, axis=-1)
    positions = jnp.arange(length, dtype=jnp.int32)
    segment = jnp.sum((positions[None, :, None] >= doc_ends[:, None, :]).astype(jnp.int32), axis=-1)
    allowed = segment[:, :, None] == segment[:, None, :]
    word_present_flag = positions[None, :] < doc_ends[:, -1:]
    return (allowed, word_present_flag)


def query_mask(query_lens, length):
    positions = jnp.arange(length, dtype=jnp.int32)
    keys_ok = positions[None, :] < query_lens[:, None]
    allowed = jnp.broadcast_to(keys_ok[:, None, :], (keys_ok.shape[0], length, length))
    return (allowed, keys_ok)


def row_scores(query_row, key_row, allowed, pos_bias):
    scores = (
        jnp.einsum("qhd,khd->hqk", query_row, key_row, preferred_element_type=jnp.float32)
        + pos_bias
    )
    return jnp.where(allowed[None], scores, excluded_entry_default)


def row_forward(query_row, key_row, value_row, allowed, pos_bias):
    length = query_row.shape[0]
    scores = row_scores(query_row, key_row, allowed, pos_bias)
    top_score = jnp.max(scores, axis=-1, keepdims=True)
    log_total = top_score + jnp.log(jnp.sum(jnp.exp(scores - top_score), axis=-1, keepdims=True))
    aggregation_factors = jnp.exp(scores - log_total).astype(jnp.bfloat16)
    mixed = jnp.einsum(
        "hqk,khd->qhd", aggregation_factors, value_row, preferred_element_type=jnp.float32
    )
    return (mixed.reshape(length, -1).astype(jnp.bfloat16), log_total)


def row_backward(query_row, key_row, value_row, allowed, log_total, dmixed_row, pos_bias):
    length, head_count, head_size = query_row.shape
    scores = row_scores(query_row, key_row, allowed, pos_bias)
    aggregation_factors = jnp.exp(scores - log_total)
    dmixed_heads = dmixed_row.reshape(length, head_count, head_size)
    dweights = jnp.einsum(
        "qhd,khd->hqk", dmixed_heads, value_row, preferred_element_type=jnp.float32
    )
    dvalue = jnp.einsum(
        "hqk,qhd->khd",
        aggregation_factors.astype(jnp.bfloat16),
        dmixed_heads,
        preferred_element_type=jnp.float32,
    )
    dscores = (
        aggregation_factors
        * (dweights - jnp.sum(aggregation_factors * dweights, axis=-1, keepdims=True))
    ).astype(jnp.bfloat16)
    dquery = jnp.einsum("hqk,khd->qhd", dscores, key_row, preferred_element_type=jnp.float32)
    dkey = jnp.einsum("hqk,qhd->khd", dscores, query_row, preferred_element_type=jnp.float32)
    return (
        dquery.reshape(length, -1).astype(jnp.bfloat16),
        dkey.reshape(length, -1).astype(jnp.bfloat16),
        dvalue.reshape(length, -1).astype(jnp.bfloat16),
        dscores.astype(jnp.float32),
    )


def on_device(
    doc_tokens,
    doc_lengths,
    query_tokens,
    query_lengths,
    candidates,
    labels,
    gain_attn,
    w_query,
    w_key,
    w_value,
    w_out,
    bias_table,
    gain_ffn,
    w_gate,
    w_up,
    w_down,
    gain_final,
    w_proj,
):
    doc_rows, doc_len, model_width = doc_tokens.shape
    query_rows, query_len = (query_tokens.shape[0], query_tokens.shape[1])
    bucket_total, head_count = bias_table.shape
    inner_width = w_query.shape[1]
    head_size = inner_width // head_count
    doc_count = doc_rows * doc_len
    table_f32 = bias_table.astype(jnp.float32)
    gain_one = gain_attn.astype(jnp.float32)
    gain_two = gain_ffn.astype(jnp.float32)
    gain_three = gain_final.astype(jnp.float32)
    inputs = jnp.concatenate(
        [doc_tokens.reshape(doc_count, model_width), query_tokens.reshape(-1, model_width)]
    ).astype(jnp.float32)
    normed_one = rms_norm(inputs, gain_one).astype(jnp.bfloat16)
    query_proj = matmul(normed_one, w_query).astype(jnp.bfloat16)
    key_proj = matmul(normed_one, w_key).astype(jnp.bfloat16)
    value_proj = matmul(normed_one, w_value).astype(jnp.bfloat16)

    def doc_heads(flat_rows):
        return flat_rows[:doc_count].reshape(doc_rows, doc_len, head_count, head_size)

    def probe_heads(flat_rows):
        return flat_rows[doc_count:].reshape(query_rows, query_len, head_count, head_size)

    doc_queries, doc_keys, doc_values = (
        doc_heads(query_proj),
        doc_heads(key_proj),
        doc_heads(value_proj),
    )
    probe_queries, probe_keys, probe_values = (
        probe_heads(query_proj),
        probe_heads(key_proj),
        probe_heads(value_proj),
    )
    doc_allowed, doc_valid = document_mask(doc_lengths, doc_len)
    probe_allowed, probe_valid = query_mask(query_lengths, query_len)
    doc_bias = relative_bias(table_f32, doc_len)
    probe_bias = relative_bias(table_f32, query_len)
    doc_mixed, doc_logsum = lax.map(
        lambda parts: row_forward(parts[0], parts[1], parts[2], parts[3], doc_bias),
        (doc_queries, doc_keys, doc_values, doc_allowed),
    )
    probe_mixed, probe_logsum = jax.vmap(row_forward, in_axes=(0, 0, 0, 0, None))(
        probe_queries, probe_keys, probe_values, probe_allowed, probe_bias
    )
    mixed = jnp.concatenate(
        [doc_mixed.reshape(doc_count, inner_width), probe_mixed.reshape(-1, inner_width)]
    )
    middle = inputs + matmul(mixed, w_out)
    normed_two = rms_norm(middle, gain_two).astype(jnp.bfloat16)
    gate_pre = matmul(normed_two, w_gate)
    upward = matmul(normed_two, w_up)
    hidden = gated_unit(gate_pre, upward).astype(jnp.bfloat16)
    output = middle + matmul(hidden, w_down)
    normed_three = rms_norm(output, gain_three).astype(jnp.bfloat16)
    projected = matmul(normed_three, w_proj)
    embedded = unit_scale(projected).astype(jnp.bfloat16)
    doc_embedded = embedded[:doc_count]
    probe_embedded = embedded[doc_count:]
    gathered = lax.all_gather(probe_embedded, "dp", axis=0, tiled=True)
    gathered_rows = gathered.shape[0]
    block_rows = 512
    block_count = gathered_rows // block_rows
    doc_blocks = doc_count // BLK
    tile_present_flag = doc_valid.reshape(doc_blocks, BLK)
    query_blocks = gathered.reshape(block_count, block_rows, -1)

    def lifted_scores(query_block):
        pairwise_match_matrix = matmul_nt(query_block, doc_embedded).reshape(
            block_rows, doc_blocks, BLK
        )
        return jnp.where(
            tile_present_flag[None],
            pairwise_match_matrix / normalizer_sharpness,
            excluded_entry_default,
        )

    def block_maxima(query_block):
        exponentiated_logit = lifted_scores(query_block)
        top_score = jnp.max(exponentiated_logit, axis=-1, keepdims=True)
        return normalizer_sharpness * (
            top_score[..., 0] + jnp.log(jnp.sum(jnp.exp(exponentiated_logit - top_score), axis=-1))
        )

    maxima = lax.map(block_maxima, query_blocks)
    received = lax.all_to_all(
        maxima.reshape(gathered_rows, doc_blocks).T, "dp", split_axis=1, concat_axis=0, tiled=True
    )
    group_blocks = received.shape[0]
    per_query = received.reshape(group_blocks, query_rows, query_len)
    chooser = (
        candidates[:, :, None] == jnp.arange(group_blocks, dtype=jnp.int32)[None, None, :]
    ).astype(jnp.float32)
    picked = jnp.einsum("acb,baq->acq", chooser, per_query, precision=highest)
    token_mask = probe_valid.astype(jnp.float32)
    logits = logit_scale * jnp.sum(picked * token_mask[:, None, :], axis=-1)
    top_logit = jnp.max(logits, axis=-1, keepdims=True)
    log_norm = top_logit + jnp.log(jnp.sum(jnp.exp(logits - top_logit), axis=-1, keepdims=True))
    label_hot = (labels[:, None] == jnp.arange(logits.shape[1], dtype=jnp.int32)[None, :]).astype(
        jnp.float32
    )
    local_loss = jnp.sum(log_norm[:, 0] - jnp.sum(logits * label_hot, axis=-1))
    dlogits = jnp.exp(logits - log_norm) - label_hot
    dpicked = (logit_scale * dlogits)[:, :, None] * token_mask[:, None, :]
    dper_query = jnp.einsum("acb,acq->baq", chooser, dpicked, precision=highest)
    returned = lax.all_to_all(
        dper_query.reshape(group_blocks, -1), "dp", split_axis=0, concat_axis=1, tiled=True
    )
    dmaxima = returned.T.reshape(block_count, block_rows, doc_blocks)

    def block_back(doc_acc, parts):
        query_block, dmax_block, tile_largest_entry = parts
        exponentiated_logit = lifted_scores(query_block)
        aggregation_factors = jnp.exp(
            exponentiated_logit - (tile_largest_entry / normalizer_sharpness)[:, :, None]
        )
        dsims = (
            (dmax_block[:, :, None] * aggregation_factors)
            .reshape(block_rows, doc_count)
            .astype(jnp.bfloat16)
        )
        return (doc_acc + matmul_tn(dsims, query_block), matmul(dsims, doc_embedded))

    doc_dembedded, dgathered = lax.scan(
        block_back, jnp.zeros(doc_embedded.shape, jnp.float32), (query_blocks, dmaxima, maxima)
    )
    probe_dembedded = lax.psum_scatter(
        dgathered.reshape(gathered_rows, -1), "dp", scatter_dimension=0, tiled=True
    )
    dembedded = jnp.concatenate([doc_dembedded, probe_dembedded])
    dprojected = jax.vjp(unit_scale, projected)[1](dembedded)[0].astype(jnp.bfloat16)
    grad_proj = matmul_tn(normed_three, dprojected)
    dnormed_three = matmul_nt(dprojected, w_proj)
    doutput, dgain_three = jax.vjp(rms_norm, output, gain_three)[1](dnormed_three)
    dbranch = doutput.astype(jnp.bfloat16)
    grad_down = matmul_tn(hidden, dbranch)
    dhidden = matmul_nt(dbranch, w_down)
    dgate_pre, dupward = jax.vjp(gated_unit, gate_pre, upward)[1](dhidden)
    dgate_pre = dgate_pre.astype(jnp.bfloat16)
    dupward = dupward.astype(jnp.bfloat16)
    grad_gate = matmul_tn(normed_two, dgate_pre)
    grad_up = matmul_tn(normed_two, dupward)
    dnormed_two = matmul_nt(dgate_pre, w_gate) + matmul_nt(dupward, w_up)
    dmiddle_part, dgain_two = jax.vjp(rms_norm, middle, gain_two)[1](dnormed_two)
    dmiddle = doutput + dmiddle_part
    dattention = dmiddle.astype(jnp.bfloat16)
    grad_out = matmul_tn(mixed, dattention)
    dmixed = matmul_nt(dattention, w_out).astype(jnp.bfloat16)
    doc_dmixed = dmixed[:doc_count].reshape(doc_rows, doc_len, inner_width)
    probe_dmixed = dmixed[doc_count:].reshape(query_rows, query_len, inner_width)

    def doc_step(bias_sum, parts):
        dquery, dkey, dvalue, dscores = row_backward(
            parts[0], parts[1], parts[2], parts[3], parts[4], parts[5], doc_bias
        )
        return (bias_sum + dscores, (dquery, dkey, dvalue))

    doc_bias_grad, doc_grads = lax.scan(
        doc_step,
        jnp.zeros((head_count, doc_len, doc_len), jnp.float32),
        (doc_queries, doc_keys, doc_values, doc_allowed, doc_logsum, doc_dmixed),
    )
    probe_grads = jax.vmap(row_backward, in_axes=(0, 0, 0, 0, 0, 0, None))(
        probe_queries,
        probe_keys,
        probe_values,
        probe_allowed,
        probe_logsum,
        probe_dmixed,
        probe_bias,
    )
    dqueries = jnp.concatenate(
        [doc_grads[0].reshape(doc_count, inner_width), probe_grads[0].reshape(-1, inner_width)]
    )
    dkeys = jnp.concatenate(
        [doc_grads[1].reshape(doc_count, inner_width), probe_grads[1].reshape(-1, inner_width)]
    )
    dvalues = jnp.concatenate(
        [doc_grads[2].reshape(doc_count, inner_width), probe_grads[2].reshape(-1, inner_width)]
    )
    grad_query = matmul_tn(normed_one, dqueries)
    grad_key = matmul_tn(normed_one, dkeys)
    grad_value = matmul_tn(normed_one, dvalues)
    dnormed_one = (
        matmul_nt(dqueries, w_query) + matmul_nt(dkeys, w_key) + matmul_nt(dvalues, w_value)
    )
    dinput_part, dgain_one = jax.vjp(rms_norm, inputs, gain_one)[1](dnormed_one)
    dinputs = dmiddle + dinput_part
    dtable = bias_gradient(doc_bias_grad, doc_len, bucket_total) + bias_gradient(
        jnp.sum(probe_grads[3], axis=0), query_len, bucket_total
    )
    all_shards = (
        lax.psum_scatter(dgain_one, ("dp", "grp"), scatter_dimension=0, tiled=True),
        lax.psum_scatter(grad_query, ("dp", "grp"), scatter_dimension=0, tiled=True),
        lax.psum_scatter(grad_key, ("dp", "grp"), scatter_dimension=0, tiled=True),
        lax.psum_scatter(grad_value, ("dp", "grp"), scatter_dimension=0, tiled=True),
        lax.psum_scatter(grad_out, ("dp", "grp"), scatter_dimension=0, tiled=True),
        lax.psum_scatter(dgain_two, ("dp", "grp"), scatter_dimension=0, tiled=True),
        lax.psum_scatter(grad_gate, ("dp", "grp"), scatter_dimension=0, tiled=True),
        lax.psum_scatter(grad_up, ("dp", "grp"), scatter_dimension=0, tiled=True),
        lax.psum_scatter(grad_down, ("dp", "grp"), scatter_dimension=0, tiled=True),
        lax.psum_scatter(dgain_three, ("dp", "grp"), scatter_dimension=0, tiled=True),
        lax.psum_scatter(grad_proj, ("dp", "grp"), scatter_dimension=0, tiled=True),
    )
    shard_one, shard_query, shard_key, shard_value, shard_out, shard_two = all_shards[:6]
    shard_gate, shard_up, shard_down, shard_three, shard_proj = all_shards[6:]
    loss_total, table_grad = lax.psum((local_loss, dtable), ("dp", "grp"))
    loss = loss_total / (query_rows * lax.axis_size("dp") * lax.axis_size("grp"))
    doc_grad = dinputs[:doc_count].reshape(doc_rows, doc_len, model_width)
    query_grad = dinputs[doc_count:].reshape(query_rows, query_len, model_width)
    return (
        loss,
        doc_grad,
        query_grad,
        shard_one,
        shard_query,
        shard_key,
        shard_value,
        shard_out,
        table_grad,
        shard_two,
        shard_gate,
        shard_up,
        shard_down,
        shard_three,
        shard_proj,
    )


def solution(mesh):
    in_specs = (
        P(("dp", "grp"), None, None),
        P(("dp", "grp"), None),
        P(("dp", "grp"), None, None),
        P(("dp", "grp")),
        P(("dp", "grp"), None),
        P(("dp", "grp")),
        P(),
        P(),
        P(),
        P(),
        P(),
        P(),
        P(),
        P(),
        P(),
        P(),
        P(),
        P(),
    )
    out_specs = (
        P(),
        P(("dp", "grp"), None, None),
        P(("dp", "grp"), None, None),
        P(("dp", "grp")),
        P(("dp", "grp"), None),
        P(("dp", "grp"), None),
        P(("dp", "grp"), None),
        P(("dp", "grp"), None),
        P(),
        P(("dp", "grp")),
        P(("dp", "grp"), None),
        P(("dp", "grp"), None),
        P(("dp", "grp"), None),
        P(("dp", "grp")),
        P(("dp", "grp"), None),
    )
    return jax.shard_map(
        on_device, mesh=mesh, in_specs=in_specs, out_specs=out_specs, check_vma=False
    )
```

profile of v0, /device:TPU:0, one launch (start us, length us, event | category | flops | bytes accessed | tf_op | source)
XLA Modules:
  0.0 1150.6 jit_solution(14113893957547625898)
XLA Ops:
  10.2 2.6 convolution_convert_fusion.2
  26.2 2.4 copy.124
  29.4 2.3 copy.125
  34.1 2.3 copy.123
  38.2 1.9 fusion.42
  41.9 1.9 reshape.458
  43.9 23.5 %while.5 = (s32[]{:T(128)}, f32[4,12,128,512]{3,1,2,0:T(8,128)}, s32[4,128,512]{2,1,0:T(8,128)}, f32[32,12]{0,1:T(8,128)}, s32[]{:T(128)}) while((s32[]{:T(128)}, f32[4,12,128,512]{3,1,2,0:T(8,128)}, s32[4,128,512]{2,1,0:T(8,128)}, f32[32,12]{0,1:T(8,128)}, s32[]{:T(128)}) %tuple.76), condition=%wide.region_4.5_spmd, body=%wide.region_3.4_spmd.sunk | while | flops 304087040 | bytes 4989005 | solution.py:55
  44.8 4.9 bitcast_dynamic-update-slice_fusion.2
  50.7 4.9 bitcast_dynamic-update-slice_fusion.2
  56.6 4.8 bitcast_dynamic-update-slice_fusion.2
  62.4 4.8 bitcast_dynamic-update-slice_fusion.2
  67.4 17.6 %copy.127 = f32[12,4,128,512]{3,2,1,0:T(8,128)} copy(f32[12,4,128,512]{3,0,2,1:T(8,128)} %bitcast.164) | data formatting | bytes 25165824 | tf_op jit(solution)/shard_map/transpose | solution.py:56
  84.9 7.8 fusion.111
  92.8 3.0 exponential_reduce_fusion
  97.3 3.5 fusion.35
  103.3 2.0 fusion.112
  105.4 4.4 multiply_convert_fusion.2
  109.8 2.1 multiply_reduce_fusion.5
  113.3 32.3 %all_gather.3 = bf16[512,128]{1,0:T(8,128)(2,1)S(1)} all-gather(bf16[64,128]{1,0:T(8,128)(2,1)S(1)} %slice.58), channel_id=1, replica_groups=mesh['dp'=8,'grp'=4] {'dp'}, dimensions={0}, use_global_device_ids=true | all-gather | bytes 147456 | tf_op jit(solution)/shard_map/all_gather | solution.py:259
  151.9 11.9 %all_to_all.35 = f32[8,1,256]{2,1,0:T(1,128)} all-to-all(f32[8,1,256]{2,1,0:T(1,128)} %reshape.462), channel_id=1, replica_groups=mesh['dp'=8,'grp'=4] {'dp'}, dimensions={0} | all-to-all | bytes 16384 | tf_op jit(solution)/shard_map/all_to_all | solution.py:285
  164.4 2.0 reduce.1
  179.6 3.9 all-to-all-start.1
  184.8 5.2 all-to-all-done.1
  190.0 2.0 reduce.2
  198.3 2.0 fusion.76
  200.4 2.1 fusion.113
  202.4 56.7 %reduce-scatter.12.cloned.1.call-done = f32[64,128]{1,0:T(8,128)} async-done(((f32[512,128]{1,0:T(8,128)}), f32[64,128]{1,0:T(8,128)}) %reduce-scatter.12.cloned.1.call-update) | async-done | bytes 32784 | tf_op jit(solution)/shard_map/reduce_scatter | solution.py:326
  263.0 2.9 fusion.102
  265.9 4.0 multiply_reduce_fusion.1
  270.7 2.5 add_add_fusion.2
  273.7 8.0 multiply_convert_fusion.1
  281.7 2.0 fusion.114
  284.5 2.9 multiply_reduce_fusion.2
  288.7 2.5 fusion.56
  291.3 2.2 convolution_convert_fusion
  295.8 6.1 fusion.38
  302.0 2.8 fusion.51
  307.8 7.2 multiply_reduce_fusion
  315.0 6.4 multiply_convert_fusion
  321.5 2.0 convolution_convert_fusion.5
  324.1 2.7 fusion.54
  328.6 4.0 convolution_convert_fusion.4
  333.4 2.7 fusion.52
  337.6 7.0 fusion.60
  345.7 6.2 fusion.116
  352.0 6.4 fusion.115
  358.5 15.4 %copy.153 = f32[12,4,128,512]{2,0,3,1:T(8,128)} copy(bf16[12,4,128,512]{3,2,1,0:T(8,128)(2,1)} %bitcast.162) | data formatting | bytes 18874368 | tf_op jit(solution)/shard_map/transpose | solution.py:63
  373.8 28.8 %while.6 = (s32[]{:T(128)}, f32[32,12]{0,1:T(8,128)S(1)}, s32[4,128,512]{1,2,0:T(8,128)}, f32[4,12,128,512]{2,1,3,0:T(8,128)}, s32[]{:T(128)}, /*index=5*/s32[]{:T(128)}) while((s32[]{:T(128)}, f32[32,12]{0,1:T(8,128)S(1)}, s32[4,128,512]{1,2,0:T(8,128)}, f32[4,12,128,512]{2,1,3,0:T(8,128)}, s32[]{:T(128)}, ...), condition=%wide.region_34.35_spmd.clone, body=%wide.region_33.34_spmd.clone.sunk | while | flops 304087808 | bytes 4983903 | solution.py:80
  374.9 6.2 fusion.166
  382.1 6.2 fusion.166
  389.3 6.2 fusion.166
  396.5 6.2 fusion.166
  403.2 2.5 fusion.55
  407.3 2.6 fusion.26
  409.9 40.7 %all-reduce.4 = (f32[]{:T(128)}, f32[768]{0:T(1024)S(1)}, f32[32,12]{0,1:T(8,128)}, f32[768]{0:T(1024)S(1)}, f32[768]{0:T(1024)S(1)}) all-reduce(f32[]{:T(128)} %get-tuple-element.246, f32[768]{0:T(1024)S(1)} %get-tuple-element.219, f32[32,12]{0,1:T(8,128)S(1)} %fusion.47, ...), channel_id=1, replica_groups=mesh['dp'=8,'grp'=4] {'dp','grp'}, use_global_device_ids=true, to_apply=%region_19.20 | all-reduce | flops 2689 | bytes 21512 | tf_op jit(solution)/shard_map/psum | solution.py:406
  450.7 2.8 fusion.28
  457.8 2.7 slice_bitcast_fusion
  460.5 8.5 reduce-scatter.20.cloned.1.call-done
  469.0 103.7 %reduce-scatter.18.cloned.1.call-done = f32[24,768]{1,0:T(8,128)} async-done(((f32[768,768]{1,0:T(8,128)}), f32[24,768]{1,0:T(8,128)}) %reduce-scatter.18.cloned.1.call-update) | async-done | bytes 73744 | tf_op jit(solution)/shard_map/reduce_scatter | solution.py:395
  572.7 104.7 %reduce-scatter.14.cloned.1.call-done = f32[24,768]{1,0:T(8,128)} async-done(((f32[768,768]{1,0:T(8,128)}), f32[24,768]{1,0:T(8,128)}) %reduce-scatter.14.cloned.1.call-update) | async-done | bytes 73744 | tf_op jit(solution)/shard_map/reduce_scatter | solution.py:393
  677.4 103.7 %reduce-scatter.16.cloned.1.call-done = f32[24,768]{1,0:T(8,128)} async-done(((f32[768,768]{1,0:T(8,128)}), f32[24,768]{1,0:T(8,128)}) %reduce-scatter.16.cloned.1.call-update) | async-done | bytes 73744 | tf_op jit(solution)/shard_map/reduce_scatter | solution.py:394
  781.1 120.5 %reduce-scatter.26.cloned.1.call-done = f32[64,768]{1,0:T(8,128)} async-done(((f32[2048,768]{1,0:T(8,128)}), f32[64,768]{1,0:T(8,128)}) %reduce-scatter.26.cloned.1.call-update) | async-done | bytes 196624 | tf_op jit(solution)/shard_map/reduce_scatter | solution.py:400
  901.6 120.0 %reduce-scatter.24.cloned.1.call-done = f32[24,2048]{1,0:T(8,128)} async-done(((f32[768,2048]{1,0:T(8,128)}), f32[24,2048]{1,0:T(8,128)}) %reduce-scatter.24.cloned.1.call-update) | async-done | bytes 196624 | tf_op jit(solution)/shard_map/reduce_scatter | solution.py:399
  1021.6 120.9 %reduce-scatter.22.cloned.1.call-done = f32[24,2048]{1,0:T(8,128)} async-done(((f32[768,2048]{1,0:T(8,128)}), f32[24,2048]{1,0:T(8,128)}) %reduce-scatter.22.cloned.1.call-update) | async-done | bytes 196624 | tf_op jit(solution)/shard_map/reduce_scatter | solution.py:398
  (308 shorter events, 88.0 us)
Async XLA Ops:
  7.2 98.2 %copy-start = (bf16[768,2048]{1,0:T(8,128)(2,1)S(1)}, bf16[768,2048]{1,0:T(8,128)(2,1)}, u32[]{:S(2)}) copy-start(bf16[768,2048]{1,0:T(8,128)(2,1)} %param.40) | copy-start | bytes 9437188
  8.0 7.7 copy-start.67
  10.2 5.6 copy-start.70
  10.2 3.6 copy-start.20
  10.2 3.6 copy-start.44
  10.2 3.6 copy-start.84
  14.8 2.8 copy-start.32
  17.6 3.7 copy-start.78
  17.6 4.3 copy-start.76
  17.6 4.9 copy-start.77
  17.6 5.5 copy-start.61
  17.7 6.1 copy-start.62
  19.3 9.3 slice-start
  26.2 5.6 slice-start.1
  92.7 4.5 copy-start.2
  92.7 4.5 copy-start.8
  95.8 5.0 copy-start.35
  97.3 3.6 copy-start.21
  97.3 3.6 copy-start.37
  97.3 3.6 copy-start.45
  97.3 3.6 copy-start.83
  102.0 3.4 copy-start.64
  102.0 7.8 copy-start.11
  102.0 3.4 copy-start.55
  105.4 4.4 copy-start.90
  105.4 4.4 copy-start.79
  112.0 34.0 %copy-start.4 = (f32[576,768]{1,0:T(8,128)}, f32[576,768]{1,0:T(8,128)S(1)}, u32[]{:S(2)}) copy-start(f32[576,768]{1,0:T(8,128)S(1)} %get-tuple-element.263) | copy-start | bytes 5308420
  112.0 34.0 %copy-start.66 = (f32[576]{0:T(1024)}, f32[576]{0:T(1024)S(1)}, u32[]{:S(2)}) copy-start(f32[576]{0:T(1024)S(1)} %get-tuple-element.262) | copy-start | bytes 6916
  112.0 33.6 %copy-start.75 = (pred[4,128]{1,0:T(4,128)(4,1)S(1)}, pred[4,128]{1,0:T(4,128)(4,1)}, u32[]{:S(2)}) copy-start(pred[4,128]{1,0:T(4,128)(4,1)} %add_compare_fusion) | copy-start | bytes 1540
  113.2 32.7 %copy-start.29 = (bf16[576,128]{1,0:T(8,128)(2,1)}, bf16[576,128]{1,0:T(8,128)(2,1)S(1)}, u32[]{:S(2)}) copy-start(bf16[576,128]{1,0:T(8,128)(2,1)S(1)} %multiply_convert_fusion.6) | copy-start | bytes 442372
  179.6 10.3 all-to-all-start.1
  183.6 75.5 %reduce-scatter.12.cloned.1.call-start = ((), (), s32[]{:S(2)}) async-start(), calls=%async_computation.11 | async-start | bytes 294912 | tf_op jit(solution)/shard_map/reduce_scatter | solution.py:326
  200.3 260.2 %reduce-scatter.28.cloned.1.call-start = ((), (), s32[]{:S(2)}) async-start(), calls=%async_computation.19 | async-start | bytes 405504
  269.9 199.0 %reduce-scatter.20.cloned.1.call-start = ((), (), s32[]{:S(2)}) async-start(), calls=%async_computation.15 | async-start | bytes 2433024 | tf_op jit(solution)/shard_map/reduce_scatter | solution.py:396
  270.7 3.0 copy-start.80
  273.2 14.3 %copy-start.13 = (f32[576,768]{1,0:T(8,128)}, f32[576,768]{1,0:T(8,128)S(1)}, u32[]{:S(2)}) copy-start(f32[576,768]{1,0:T(8,128)S(1)} %add_add_fusion.2) | copy-start | bytes 5308420
  273.7 8.0 copy-start.82
  281.7 2.9 copy-start.12
  281.7 2.9 copy-start.54
  281.7 2.9 copy-start.56
  284.5 2.9 copy-start.65
  291.2 281.5 %reduce-scatter.18.cloned.1.call-start = ((), (), s32[]{:S(2)}) async-start(), calls=%async_computation.14 | async-start | bytes 2433024 | tf_op jit(solution)/shard_map/reduce_scatter | solution.py:395
  294.8 7.1 copy-start.49
  295.8 6.1 copy-start.22
  295.8 6.1 copy-start.46
  295.8 6.1 copy-start.68
  295.8 6.1 copy-start.71
  301.9 2.9 copy-start.39
  304.8 3.0 copy-start.9
  304.8 372.6 %reduce-scatter.14.cloned.1.call-start = ((), (), s32[]{:S(2)}) async-start(), calls=%async_computation.12 | async-start | bytes 2433024 | tf_op jit(solution)/shard_map/reduce_scatter | solution.py:393
  315.0 6.5 copy-start.10
  324.1 2.7 copy-start.42
  326.8 454.3 %reduce-scatter.16.cloned.1.call-start = ((), (), s32[]{:S(2)}) async-start(), calls=%async_computation.13 | async-start | bytes 2433024 | tf_op jit(solution)/shard_map/reduce_scatter | solution.py:394
  328.5 4.9 copy-start.47
  328.5 4.9 copy-start.69
  328.5 4.9 copy-start.72
  336.1 565.4 %reduce-scatter.26.cloned.1.call-start = ((), (), s32[]{:S(2)}) async-start(), calls=%async_computation.18 | async-start | bytes 6488064 | tf_op jit(solution)/shard_map/reduce_scatter | solution.py:400
  344.6 677.0 %reduce-scatter.24.cloned.1.call-start = ((), (), s32[]{:S(2)}) async-start(), calls=%async_computation.17 | async-start | bytes 6488064 | tf_op jit(solution)/shard_map/reduce_scatter | solution.py:399
  352.0 790.5 %reduce-scatter.22.cloned.1.call-start = ((), (), s32[]{:S(2)}) async-start(), calls=%async_computation.16 | async-start | bytes 6488064 | tf_op jit(solution)/shard_map/reduce_scatter | solution.py:398
  373.8 28.8 %copy-start.48 = (f32[12,32,32]{1,2,0:T(8,128)S(1)}, f32[12,32,32]{1,2,0:T(8,128)}, u32[]{:S(2)}) copy-start(f32[12,32,32]{1,2,0:T(8,128)} %get-tuple-element.244) | copy-start | bytes 147460
  373.8 28.8 %copy-start.63 = (s32[32,32]{0,1:T(8,128)S(1)}, s32[32,32]{0,1:T(8,128)}, u32[]{:S(2)}) copy-start(s32[32,32]{0,1:T(8,128)} %constant.165.clone) | copy-start | bytes 12292
  373.8 29.3 %copy-start.43 = (bf16[12,64,512]{2,1,0:T(8,128)(2,1)S(1)}, bf16[12,64,512]{2,1,0:T(8,128)(2,1)}, u32[]{:S(2)}) copy-start(bf16[12,64,512]{2,1,0:T(8,128)(2,1)} %copy-done.42) | copy-start | bytes 2359300
  407.3 43.4 %copy-start.59 = (f32[576]{0:T(1024)S(1)}, f32[576]{0:T(1024)}, u32[]{:S(2)}) copy-start(f32[576]{0:T(1024)} %copy-done.58) | copy-start | bytes 6916
  450.7 691.8 %copy-start.1 = (bf16[768,2048]{1,0:T(8,128)(2,1)S(1)}, bf16[768,2048]{1,0:T(8,128)(2,1)}, u32[]{:S(2)}) copy-start(bf16[768,2048]{1,0:T(8,128)(2,1)} %param.40) | copy-start | bytes 9437188
  (41 other events, 64.8 us)
Sparse Core Ops, SparseCore 0:
  200.4 58.6 reduce-scatter.11
  270.1 93.9 reduce-scatter.27
  370.8 98.1 reduce-scatter.19
  474.7 97.9 reduce-scatter.17
  579.3 98.0 reduce-scatter.13
  683.1 97.9 reduce-scatter.15
  788.2 113.2 reduce-scatter.25
  907.8 113.7 reduce-scatter.23
  1028.7 113.6 reduce-scatter.21
where the time goes:
time: 1160 us; the launch traced here: 1150 us
  waiting for transfers between devices  744 us (64%)
  matrix products  160 us (14%)
  local copies, waits for them, and re-layouts  101 us (9%)
  blocking collectives  84.9 us (7%)
  other arithmetic  38.8 us (3%)
  between operations  17.3 us (1%)
    reduce_scatter x1, waiting for transfers between devices, on_device(): lax.psum_scatter(grad_gate, ('dp', 'grp'), scatter_dimension=0, tiled=True)  121 us
    reduce_scatter x1, waiting for transfers between devices, on_device(): lax.psum_scatter(grad_down, ('dp', 'grp'), scatter_dimension=0, tiled=True)  120 us
    reduce_scatter x1, waiting for transfers between devices, on_device(): lax.psum_scatter(grad_up, ('dp', 'grp'), scatter_dimension=0, tiled=True)  120 us
    reduce_scatter x1, waiting for transfers between devices, on_device(): lax.psum_scatter(grad_query, ('dp', 'grp'), scatter_dimension=0, tiled=True)  105 us
    reduce_scatter x1, waiting for transfers between devices, on_device(): lax.psum_scatter(grad_key, ('dp', 'grp'), scatter_dimension=0, tiled=True)  104 us
    reduce_scatter x1, waiting for transfers between devices, on_device(): lax.psum_scatter(grad_value, ('dp', 'grp'), scatter_dimension=0, tiled=True)  104 us
    reduce_scatter x1, waiting for transfers between devices, on_device(): lax.psum_scatter(dgathered.reshape(gathered_rows, -1), 'dp', scatter_dime...  56.7 us
    psum x1, blocking collectives, on_device(): loss_total, table_grad = lax.psum((local_loss, dtable), ('dp', 'grp'))  40.7 us
  transfers between devices with their start and end apart: 10, of which 9 were waited for; matrix products, arithmetic and copies ran while one was open for 12% of the time, Pallas kernels for 0%

commit v1 on v0

v1 whole, which is shorter than its diff:
```python
import functools
import math

import jax
import jax.numpy as jnp
import numpy as np
from jax import lax
from jax.experimental import pallas as pl
from jax.experimental.pallas import tpu as pltpu
from jax.sharding import PartitionSpec as P

F32, BF16 = jnp.float32, jnp.bfloat16
BUCKETS = 32
DIST = 128
BLK = 128
EPS = 1e-6
SHARP = 0.25
SCALE = 16.0
NEG = -1e30
GELU_A = math.sqrt(2.0 / math.pi)
GELU_B = 0.044715
SPAN = 512
CH = 512
LANE = 128
PACK_INT = 48
highest = lax.Precision.HIGHEST


def nn(a, b):
    return jnp.dot(a, b, preferred_element_type=F32)


def nt(a, b):
    return lax.dot_general(a, b, (((1,), (1,)), ((), ())), preferred_element_type=F32)


def tn(a, b):
    return lax.dot_general(a, b, (((0,), (0,)), ((), ())), preferred_element_type=F32)


def bucket_of(offsets):
    half = BUCKETS // 2
    exact = half // 2
    dist = np.abs(offsets)
    scaled = np.log(np.maximum(dist, 1) / exact) / np.log(DIST / exact) * (half - exact)
    far = np.minimum(exact + np.maximum(scaled, 0).astype(np.int64), half - 1)
    return (offsets > 0) * half + np.where(dist < exact, dist, far)


def strip_onehot():
    j = np.arange(SPAN)
    offset = np.where(j < 384, 128 - j, 640 - j)
    index = np.stack([bucket_of(offset[(j - r) % SPAN]) for r in range(8)]).reshape(-1)
    return (index[None, :] == np.arange(BUCKETS)[:, None]).astype(np.float32)


VM = pl.BlockSpec(memory_space=pltpu.VMEM)
SM = pl.BlockSpec(memory_space=pltpu.SMEM)
HB = pl.BlockSpec(memory_space=pl.ANY)


def shape_of(shape, dtype):
    return jax.ShapeDtypeStruct(shape, dtype)


def call(kernel, name, outs, args, specs, scratch, mib, flops, moved=8 << 20):
    return pl.pallas_call(
        kernel,
        name=name,
        out_shape=outs,
        in_specs=specs,
        out_specs=[VM] * len(outs),
        scratch_shapes=scratch,
        compiler_params=pltpu.CompilerParams(vmem_limit_bytes=mib << 20),
        cost_estimate=pl.CostEstimate(flops=int(flops), bytes_accessed=int(moved), transcendentals=0),
    )(*args)


def fetch(pairs, sems):
    copies = []
    for i, (src, dst) in enumerate(pairs):
        copy = pltpu.make_async_copy(src, dst, sems.at[i])
        copy.start()
        copies.append(copy)
    return copies


def half_lanes(values, side):
    lane = lax.broadcasted_iota(jnp.int32, (1, LANE), 1)
    return jnp.where((lane // 64) == side, values.astype(F32), 0.0).astype(BF16)


def norm_back(values, gain, dn):
    s = lax.rsqrt(jnp.mean(values * values, axis=-1, keepdims=True) + EPS)
    unit = values * s
    t = dn * gain
    dv = s * (t - unit * jnp.mean(t * unit, axis=-1, keepdims=True))
    return dv, jnp.sum(dn * unit, axis=0, keepdims=True)


def forward_kernel(
    is_doc, x_ref, lens_ref, gains_ref, extra_ref, wq, wk, wv, wo, wg, wu, wd, wp,
    q_ref, k_ref, v_ref, e_ref, il_ref, mixt_ref, mid_ref, n1_ref, n2_ref, hid_ref, a_ref, b_ref,
    out_ref, n3_ref, proj_ref, emb_ref, *rest,
):
    if is_doc:
        base_ref, tail = extra_ref, rest
    else:
        tab_ref, hot_ref, ints_ref = extra_ref
        base_ref, tail = rest[0], rest[1:]
    wq_s, wk_s, wv_s, wo_s, wg_s, wu_s, wd_s, wp_s, mask_s, strip_s, s_s, vt_s, sems = tail
    tokens, width = x_ref.shape
    hidden = wg.shape[1]
    copies = fetch(
        ((wq, wq_s), (wk, wk_s), (wv, wv_s), (wo, wo_s), (wg, wg_s), (wu, wu_s), (wd, wd_s), (wp, wp_s)), sems
    )
    heads = e_ref.shape[0]
    if not is_doc:
        for r in range(8):
            rows = tn(tab_ref[...], hot_ref[:, r * SPAN:(r + 1) * SPAN])
            for h in range(heads):
                base_ref[h, r:r + 1, :] = rows[h:h + 1, :]
    x = x_ref[...].astype(F32)
    s1 = lax.rsqrt(jnp.mean(x * x, axis=-1, keepdims=True) + EPS)
    n1_ref[...] = (x * s1 * gains_ref[0:1, :]).astype(BF16)
    tile = min(tokens, 128)
    wide = min(tokens, 256)
    blocks = tokens // tile
    row_id = lax.broadcasted_iota(jnp.int32, (tokens, 1), 0)
    col_id = lax.broadcasted_iota(jnp.int32, (1, tokens), 1)
    if is_doc:
        seg_k = jnp.zeros((tokens, 1), jnp.int32)
        seg_q = jnp.zeros((1, tokens), jnp.int32)
        end = jnp.int32(0)
        for i in range(lens_ref.shape[1]):
            end = end + lens_ref[0, i]
            seg_k = seg_k + (row_id >= end).astype(jnp.int32)
            seg_q = seg_q + (col_id >= end).astype(jnp.int32)
    else:
        count = lens_ref.shape[0]
        length = tokens // count
        seg_q = col_id // length
        seg_k = jnp.full((tokens, 1), -1, jnp.int32)
        for i in range(count):
            inside = (row_id >= i * length) & (row_id < i * length + lens_ref[i])
            seg_k = jnp.where(inside, i, seg_k)
    mask_s[...] = jnp.where(seg_k == seg_q, 0.0, NEG)
    for i, (w, o) in enumerate(((wq_s, q_ref), (wk_s, k_ref), (wv_s, v_ref))):
        copies[i].wait()
        o[...] = nn(n1_ref[...], w[...]).astype(BF16)
    vt_s[...] = v_ref[...].T

    def pair_body(p, carry):
        col = pl.ds(pl.multiple_of(p * LANE, LANE), LANE)
        for s in range(2):
            h = 2 * p + s
            first = base_ref[h]
            for g in range(tile // 8):
                strip_s[8 * g:8 * g + 8, :] = pltpu.roll(first, 8 * g, 1) if g else first
            low_far, high_far = first[0:1, 256:256 + tile], first[0:1, 384:384 + tile]
            kp = half_lanes(k_ref[:, col], s)
            rows = pl.ds(pl.multiple_of(p * LANE + 64 * s, 64), 64)
            for qc in range(tokens // wide):
                cols = slice(qc * wide, (qc + 1) * wide)
                qp = q_ref[cols, col]
                top = None
                for kb in range(blocks):
                    ks = slice(kb * tile, (kb + 1) * tile)
                    scores = nt(kp[ks], qp)
                    tops = []
                    for qs in range(wide // tile):
                        qb = qc * (wide // tile) + qs
                        d = kb - qb
                        t = scores[:, qs * tile:(qs + 1) * tile]
                        if abs(d) <= 1:
                            lo = (1 - d) * 128
                            t = t + strip_s[:, lo:lo + tile]
                        else:
                            t = t + (high_far if d > 0 else low_far)
                        t = t + mask_s[ks, qb * tile:(qb + 1) * tile]
                        s_s[ks, qs * tile:(qs + 1) * tile] = t
                        tops.append(jnp.max(t, axis=0, keepdims=True))
                    mk = jnp.concatenate(tops, axis=1) if len(tops) > 1 else tops[0]
                    top = mk if top is None else jnp.maximum(top, mk)
                total = None
                for kb in range(blocks):
                    ks = slice(kb * tile, (kb + 1) * tile)
                    e = jnp.exp(s_s[ks, :] - top)
                    part = jnp.sum(e, axis=0, keepdims=True)
                    total = part if total is None else total + part
                    e_ref[h, ks, cols] = e.astype(BF16)
                inverse = 1.0 / total
                il_ref[h, :, cols] = inverse
                o = nn(vt_s[rows, :], e_ref[h, :, cols])
                mixt_ref[rows, cols] = (o * inverse).astype(BF16)
        return carry

    lax.fori_loop(0, width // LANE, pair_body, 0)
    copies[3].wait()
    mid_ref[...] = x_ref[...].astype(F32) + nn(mixt_ref[...].T, wo_s[...])
    mid = mid_ref[...]
    s2 = lax.rsqrt(jnp.mean(mid * mid, axis=-1, keepdims=True) + EPS)
    n2_ref[...] = (mid * s2 * gains_ref[1:2, :]).astype(BF16)
    copies[4].wait()
    copies[5].wait()

    def ff_body(j, carry):
        col = pl.ds(pl.multiple_of(j * CH, CH), CH)
        g = nn(n2_ref[...], wg_s[:, col])
        u = nn(n2_ref[...], wu_s[:, col])
        sq = g * g
        t = jnp.tanh(GELU_A * g * (1.0 + GELU_B * sq))
        half = 0.5 + 0.5 * t
        gel = g * half
        slope = half + (0.5 * GELU_A) * g * (1.0 - t * t) * (1.0 + 3.0 * GELU_B * sq)
        hid_ref[:, col] = (gel * u).astype(BF16)
        a_ref[:, col] = (u * slope).astype(BF16)
        b_ref[:, col] = gel.astype(BF16)
        return carry

    lax.fori_loop(0, hidden // CH, ff_body, 0)
    copies[6].wait()
    out_ref[...] = mid_ref[...] + nn(hid_ref[...], wd_s[...])
    o = out_ref[...]
    s3 = lax.rsqrt(jnp.mean(o * o, axis=-1, keepdims=True) + EPS)
    n3_ref[...] = (o * s3 * gains_ref[2:3, :]).astype(BF16)
    copies[7].wait()
    pr = nn(n3_ref[...], wp_s[...])
    proj_ref[...] = pr
    emb = (pr * lax.rsqrt(jnp.sum(pr * pr, axis=-1, keepdims=True) + EPS)).astype(BF16)
    if is_doc:
        emb_ref[...] = emb
    else:
        emb_ref[0:tokens, :] = emb
        emb_ref[tokens:, :] = ints_ref[...]


def forward(x, lens, gains, extra, weights, is_doc, heads):
    tokens, width = x.shape
    hidden = weights[4].shape[1]
    proj = weights[7].shape[1]
    outs = [shape_of((tokens, width), BF16)] * 3 + [
        shape_of((heads, tokens, tokens), BF16),
        shape_of((heads, 1, tokens), F32),
        shape_of((width, tokens), BF16),
        shape_of((tokens, width), F32),
        shape_of((tokens, width), BF16),
        shape_of((tokens, width), BF16),
        shape_of((tokens, hidden), BF16),
        shape_of((tokens, hidden), BF16),
        shape_of((tokens, hidden), BF16),
        shape_of((tokens, width), F32),
        shape_of((tokens, width), BF16),
        shape_of((tokens, proj), F32),
        shape_of((tokens + (0 if is_doc else PACK_INT), proj), BF16),
    ]
    tile = min(tokens, 128)
    scratch = [pltpu.VMEM(w.shape, BF16) for w in weights] + [
        pltpu.VMEM((tokens, tokens), F32),
        pltpu.VMEM((tile, SPAN), F32),
        pltpu.VMEM((tokens, min(tokens, 256)), F32),
        pltpu.VMEM((width, tokens), BF16),
        pltpu.SemaphoreType.DMA((8,)),
    ]
    if is_doc:
        kernel = functools.partial(forward_kernel, True)
        args, specs = [x, lens, gains, extra, *weights], [VM, SM, VM, VM] + [HB] * 8
    else:
        outs.append(shape_of((heads, 8, SPAN), F32))

        def kernel(x_ref, lens_ref, gains_ref, tab_ref, hot_ref, ints_ref, *rest):
            forward_kernel(False, x_ref, lens_ref, gains_ref, (tab_ref, hot_ref, ints_ref), *rest)

        args, specs = [x, lens, gains, *extra, *weights], [VM, SM, VM, VM, VM, VM] + [HB] * 8
    flops = 2 * tokens * (4 * width * width + 3 * width * hidden + width * proj) + 4 * tokens * tokens * width
    return call(
        kernel, "doc_forward" if is_doc else "query_forward", outs, args, specs, scratch, 58, flops, 30 << 20
    )


def unpack(got_ref, tokens):
    parts = got_ref.shape[0]
    own = 2
    lane = lax.broadcasted_iota(jnp.int32, (1, LANE), 1)
    ints = None
    for i in range(parts):
        block = got_ref[i, tokens:, :].astype(F32)
        if i:
            block = pltpu.roll(block, own * i, 1)
        block = jnp.where((lane // own) == i, block, 0.0)
        ints = block if ints is None else ints + block
    return ints[0:32, :], ints[32:33, :], ints[33:34, :]


def expand_onehot(queries, length):
    col = lax.broadcasted_iota(jnp.int32, (LANE, queries * length), 1)
    row = lax.broadcasted_iota(jnp.int32, (LANE, queries * length), 0)
    return ((col // length) == row).astype(F32)


def token_valid(lens, queries, length):
    hot = expand_onehot(queries, length)
    spread = jnp.dot(jnp.broadcast_to(lens, (8, LANE)), hot, precision=highest, preferred_element_type=F32)[0:1]
    place = lax.broadcasted_iota(jnp.int32, (1, queries * length), 1) % length
    return place.astype(F32) < spread, hot


def total_length(lens_ref):
    end = jnp.int32(0)
    for i in range(lens_ref.shape[1]):
        end = end + lens_ref[0, i]
    return end


def block_scores(emb_ref, q_s, b, end):
    t = nt(emb_ref[b * BLK:(b + 1) * BLK, :], q_s[...]) * (1.0 / SHARP)
    row = lax.broadcasted_iota(jnp.int32, (BLK, 1), 0) + b * BLK
    return jnp.where(row < end, t, NEG)


def score_kernel(length, got_ref, emb_ref, lens_ref, sums_ref, lse_ref, q_s):
    parts = got_ref.shape[0]
    tokens = q_s.shape[0] // parts
    queries = q_s.shape[0] // length
    for i in range(parts):
        q_s[i * tokens:(i + 1) * tokens, :] = got_ref[i, 0:tokens, :]
    _, _, lens = unpack(got_ref, tokens)
    valid, hot = token_valid(lens, queries, length)
    end = total_length(lens_ref)
    blocks = emb_ref.shape[0] // BLK
    rows = []
    for b in range(blocks):
        t = block_scores(emb_ref, q_s, b, end)
        top = jnp.max(t, axis=0, keepdims=True)
        lse = top + jnp.log(jnp.sum(jnp.exp(t - top), axis=0, keepdims=True))
        lse_ref[b:b + 1, :] = lse
        rows.append(jnp.where(valid, SHARP * lse, 0.0))
    rows.append(jnp.zeros((8 - blocks, rows[0].shape[1]), F32))
    sums = lax.dot_general(
        jnp.concatenate(rows, axis=0), hot, (((1,), (1,)), ((), ())), precision=highest, preferred_element_type=F32
    )
    for i in range(parts):
        sums_ref[i] = sums


def scores(got, emb, lens, length):
    parts = got.shape[0]
    tokens = got.shape[1] - PACK_INT
    total = parts * tokens
    return call(
        functools.partial(score_kernel, length),
        "block_sums",
        [shape_of((parts, 8, LANE), F32), shape_of((8, total), F32)],
        [got, emb, lens],
        [VM, VM, SM],
        [pltpu.VMEM((total, emb.shape[1]), BF16)],
        24,
        2 * emb.shape[0] * total * 128,
        1 << 20,
    )


def loss_kernel(length, got_ref, sums_ref, emb_ref, lse_ref, lens_ref, me_ref, doc_ref, qry_ref, loss_ref, q_s, d_s, s_s):
    parts = got_ref.shape[0]
    tokens = q_s.shape[0] // parts
    queries = q_s.shape[0] // length
    for i in range(parts):
        q_s[i * tokens:(i + 1) * tokens, :] = got_ref[i, 0:tokens, :]
    cand, label, lens = unpack(got_ref, tokens)
    valid, hot = token_valid(lens, queries, length)
    blocks = emb_ref.shape[0] // BLK
    logits = jnp.zeros(cand.shape, F32)
    for i in range(parts):
        for b in range(blocks):
            logits = logits + jnp.where(cand == float(i * blocks + b), sums_ref[i, b:b + 1, :], 0.0)
    logits = SCALE * logits
    top = jnp.max(logits, axis=0, keepdims=True)
    lse = top + jnp.log(jnp.sum(jnp.exp(logits - top), axis=0, keepdims=True))
    choice = lax.broadcasted_iota(jnp.int32, cand.shape, 0).astype(F32) == label
    lane = lax.broadcasted_iota(jnp.int32, (1, LANE), 1)
    picked = jnp.sum(jnp.where(choice, logits, 0.0), axis=0, keepdims=True)
    each = jnp.where(lane < queries, lse - picked, 0.0)
    loss_ref[...] = jnp.broadcast_to(jnp.sum(each, axis=1, keepdims=True), (1, LANE))
    dlogits = SCALE * (jnp.exp(logits - lse) - jnp.where(choice, 1.0, 0.0))
    rows = []
    for b in range(blocks):
        mine = (me_ref[0] * blocks + b).astype(F32)
        rows.append(jnp.sum(jnp.where(cand == mine, dlogits, 0.0), axis=0, keepdims=True))
    rows.append(jnp.zeros((8 - blocks, LANE), F32))
    spread = jnp.dot(jnp.concatenate(rows, axis=0), hot, precision=highest, preferred_element_type=F32)
    end = total_length(lens_ref)
    for b in range(blocks):
        t = block_scores(emb_ref, q_s, b, end)
        weight = jnp.where(valid, spread[b:b + 1, :], 0.0)
        d_s[b * BLK:(b + 1) * BLK, :] = (weight * jnp.exp(t - lse_ref[b:b + 1, :])).astype(BF16)
    doc_ref[...] = nn(d_s[...], q_s[...])
    s_s[...] = d_s[...].T
    qry_ref[...] = nn(s_s[...], emb_ref[...]).reshape(qry_ref.shape)


def retrieval_back(got, sums, emb, lse, lens, me, length):
    parts = got.shape[0]
    tokens = got.shape[1] - PACK_INT
    total = parts * tokens
    docs, proj = emb.shape
    return call(
        functools.partial(loss_kernel, length),
        "retrieval_back",
        [shape_of((docs, proj), F32), shape_of((parts, tokens, proj), F32), shape_of((1, LANE), F32)],
        [got, sums, emb, lse, lens, me],
        [VM, VM, VM, VM, SM, SM],
        [pltpu.VMEM((total, proj), BF16), pltpu.VMEM((docs, total), BF16), pltpu.VMEM((total, docs), BF16)],
        32,
        6 * docs * total * proj,
        2 << 20,
    )


def chain_kernel(
    demb_ref, proj_ref, out_ref, mid_ref, a_ref, b_ref, gains_ref, wp, wd, wg, wu, wo,
    dpj_ref, dbr_ref, dg_ref, du_ref, datt_ref, dmid_ref, dmix_ref, dmixt_ref, dgain_ref,
    wp_s, wd_s, wg_s, wu_s, wo_s, acc_s, sems,
):
    copies = fetch(((wp, wp_s), (wd, wd_s), (wg, wg_s), (wu, wu_s), (wo, wo_s)), sems)
    hidden = a_ref.shape[1]
    if len(demb_ref.shape) == 3:
        dy = demb_ref[0]
        for i in range(1, demb_ref.shape[0]):
            dy = dy + demb_ref[i]
    else:
        dy = demb_ref[...]
    pr = proj_ref[...]
    r = lax.rsqrt(jnp.sum(pr * pr, axis=-1, keepdims=True) + EPS)
    unit = pr * r
    dpj_ref[...] = (r * (dy - unit * jnp.sum(dy * unit, axis=-1, keepdims=True))).astype(BF16)
    copies[0].wait()
    dn3 = nt(dpj_ref[...], wp_s[...])
    dout, dgain3 = norm_back(out_ref[...], gains_ref[2:3, :], dn3)
    dgain_ref[1:2, :] = dgain3
    dmid_ref[...] = dout
    dbr_ref[...] = dout.astype(BF16)
    acc_s[...] = jnp.zeros_like(acc_s)
    for i in range(1, 4):
        copies[i].wait()

    def body(j, carry):
        col = pl.ds(pl.multiple_of(j * CH, CH), CH)
        dh = nt(dbr_ref[...], wd_s[col, :])
        dg = (dh * a_ref[:, col].astype(F32)).astype(BF16)
        du = (dh * b_ref[:, col].astype(F32)).astype(BF16)
        dg_ref[:, col] = dg
        du_ref[:, col] = du
        acc_s[...] += nt(dg, wg_s[:, col]) + nt(du, wu_s[:, col])
        return carry

    lax.fori_loop(0, hidden // CH, body, 0)
    dpart, dgain2 = norm_back(mid_ref[...], gains_ref[1:2, :], acc_s[...])
    dgain_ref[0:1, :] = dgain2
    dmid = dmid_ref[...] + dpart
    dmid_ref[...] = dmid
    datt_ref[...] = dmid.astype(BF16)
    copies[4].wait()
    dmix = nt(datt_ref[...], wo_s[...]).astype(BF16)
    dmix_ref[...] = dmix
    dmixt_ref[...] = dmix.T


def chain(demb, proj, out, mid, a, b, gains, wp, wd, wg, wu, wo, name):
    tokens, width = out.shape
    hidden = a.shape[1]
    weights = (wp, wd, wg, wu, wo)
    return call(
        chain_kernel,
        name,
        [
            shape_of(proj.shape, BF16),
            shape_of((tokens, width), BF16),
            shape_of((tokens, hidden), BF16),
            shape_of((tokens, hidden), BF16),
            shape_of((tokens, width), BF16),
            shape_of((tokens, width), F32),
            shape_of((tokens, width), BF16),
            shape_of((width, tokens), BF16),
            shape_of((2, width), F32),
        ],
        [demb, proj, out, mid, a, b, gains, *weights],
        [VM] * 7 + [HB] * 5,
        [pltpu.VMEM(w.shape, BF16) for w in weights]
        + [pltpu.VMEM((tokens, width), F32), pltpu.SemaphoreType.DMA((5,))],
        56,
        2 * tokens * (width * width + 3 * width * hidden + width * 128),
        30 << 20,
    )


def attention_back_kernel(
    q_ref, k_ref, v_ref, e_ref, il_ref, mixt_ref, dmix_ref, dmixt_ref, dqkv_ref, diag_ref, far_ref,
    kt_s, dqt_s, p_s, ds_s, strip_s, dk_s, dv_s,
):
    tokens, width = q_ref.shape
    tile = min(tokens, 128)
    wide = min(tokens, 256)
    blocks = tokens // tile
    kt_s[...] = k_ref[...].T

    def pair_body(p, carry):
        col = pl.ds(pl.multiple_of(p * LANE, LANE), LANE)
        for s in range(2):
            h = 2 * p + s
            vp = half_lanes(v_ref[:, col], s)
            dm = half_lanes(dmix_ref[:, col], s)
            qm = half_lanes(q_ref[:, col], s)
            rows = pl.ds(pl.multiple_of(p * LANE + 64 * s, 64), 64)
            strip_s[...] = jnp.zeros_like(strip_s)
            far_low = jnp.zeros((8, LANE), F32)
            far_high = jnp.zeros((8, LANE), F32)
            for qc in range(tokens // wide):
                cols = slice(qc * wide, (qc + 1) * wide)
                dt = dmixt_ref[col, cols]
                delta = jnp.sum(
                    dmixt_ref[rows, cols].astype(F32) * mixt_ref[rows, cols].astype(F32), axis=0, keepdims=True
                )
                inverse = il_ref[h, :, cols]
                for kb in range(blocks):
                    ks = slice(kb * tile, (kb + 1) * tile)
                    dp = nn(vp[ks], dt)
                    prob = e_ref[h, ks, cols].astype(F32) * inverse
                    p_s[ks, :] = prob.astype(BF16)
                    ds = (prob * (dp - delta)).astype(BF16)
                    ds_s[ks, :] = ds
                    kept = ds.astype(F32)
                    for qs in range(wide // tile):
                        d = kb - (qc * (wide // tile) + qs)
                        t = kept[:, qs * tile:(qs + 1) * tile]
                        if abs(d) <= 1:
                            lo = (1 - d) * 128
                            strip_s[0:tile, lo:lo + tile] += t
                        else:
                            part = t[0:8]
                            for g in range(1, tile // 8):
                                part = part + t[8 * g:8 * g + 8]
                            if d > 0:
                                far_high = far_high + part
                            else:
                                far_low = far_low + part
                dv = nn(p_s[...], dm[cols])
                dk = nn(ds_s[...], qm[cols])
                if s == 0 and qc == 0:
                    dv_s[...] = dv
                    dk_s[...] = dk
                else:
                    dv_s[...] += dv
                    dk_s[...] += dk
                dqt_s[rows, cols] = nn(kt_s[rows, :], ds_s[...]).astype(BF16)
            fold = strip_s[...]
            size = strip_s.shape[0]
            while size > 8:
                size //= 2
                fold = fold[:size] + pltpu.roll(fold[size:], SPAN - size, 1)
            diag_ref[h] = fold
            far_ref[h, 0:8, :] = far_low
            far_ref[h, 8:16, :] = far_high
        kcol = pl.ds(pl.multiple_of(width + p * LANE, LANE), LANE)
        vcol = pl.ds(pl.multiple_of(2 * width + p * LANE, LANE), LANE)
        dqkv_ref[:, kcol] = dk_s[...].astype(BF16)
        dqkv_ref[:, vcol] = dv_s[...].astype(BF16)
        return carry

    lax.fori_loop(0, width // LANE, pair_body, 0)
    dqkv_ref[:, 0:width] = dqt_s[...].T


def attention_back(q, k, v, e, il, mixt, dmix, dmixt, name):
    tokens, width = q.shape
    heads = e.shape[0]
    tile, wide = min(tokens, 128), min(tokens, 256)
    return call(
        attention_back_kernel,
        name,
        [
            shape_of((tokens, 3 * width), BF16),
            shape_of((heads, 8, SPAN), F32),
            shape_of((heads, 16, LANE), F32),
        ],
        [q, k, v, e, il, mixt, dmix, dmixt],
        [VM] * 8,
        [
            pltpu.VMEM((width, tokens), BF16),
            pltpu.VMEM((width, tokens), BF16),
            pltpu.VMEM((tokens, wide), BF16),
            pltpu.VMEM((tokens, wide), BF16),
            pltpu.VMEM((tile, SPAN), F32),
            pltpu.VMEM((tokens, LANE), F32),
            pltpu.VMEM((tokens, LANE), F32),
        ],
        40,
        10 * tokens * tokens * width,
        16 << 20,
    )


def input_kernel(dqkv_ref, dmid_ref, x_ref, gains_ref, wq, wk, wv, dx_ref, dgain_ref, wq_s, wk_s, wv_s, sems):
    copies = fetch(((wq, wq_s), (wk, wk_s), (wv, wv_s)), sems)
    width = x_ref.shape[1]
    total = None
    for i, w in enumerate((wq_s, wk_s, wv_s)):
        copies[i].wait()
        part = nt(dqkv_ref[:, i * width:(i + 1) * width], w[...])
        total = part if total is None else total + part
    dv, dgain = norm_back(x_ref[...].astype(F32), gains_ref[0:1, :], total)
    dx_ref[...] = dmid_ref[...] + dv
    dgain_ref[...] = dgain


def input_back(dqkv, dmid, x, gains, wq, wk, wv, name):
    tokens, width = x.shape
    return call(
        input_kernel,
        name,
        [shape_of((tokens, width), F32), shape_of((1, width), F32)],
        [dqkv, dmid, x, gains, wq, wk, wv],
        [VM] * 4 + [HB] * 3,
        [pltpu.VMEM(wq.shape, BF16)] * 3 + [pltpu.SemaphoreType.DMA((3,))],
        32,
        6 * tokens * width * width,
        8 << 20,
    )


def put_rows(own_ref, send_ref, core, acc_s, per, offset, lanes, pad=0, extra=None):
    count = own_ref.shape[0]
    for j in range(count):
        for ref, side in ((own_ref, core), (send_ref, 1 - core)):
            rows = pl.ds(pl.multiple_of(2 * per * j + per * side, 8), per)
            pieces = [acc_s[rows, lo:lo + 256] for lo in lanes]
            if extra is not None:
                pieces.append(extra(rows))
            if pad:
                pieces.append(jnp.zeros((pad, 256), F32))
            block = jnp.concatenate(pieces, axis=0) if len(pieces) > 1 else pieces[0]
            ref[j, pl.ds(offset, block.shape[0]), :] = block.astype(BF16)


def ff_grad_kernel(
    core_ref, n2_ref, n2q_ref, hid_ref, hidq_ref, n3_ref, n3q_ref, mixt_ref, mixtq_ref,
    dg_ref, dgq_ref, du_ref, duq_ref, dbr_ref, dbrq_ref, dpj_ref, dpjq_ref, datt_ref, dattq_ref,
    own_ref, send_ref, n2t_s, n2tq_s, hidt_s, hidtq_s, acc_s, accd_s, accp_s,
):
    core = core_ref[0]
    width = n2_ref.shape[1]
    hidden = hid_ref.shape[1]
    count = own_ref.shape[0]
    per, per_down = width // (2 * count), hidden // (2 * count)
    hidt_s[...] = hid_ref[...].T
    hidtq_s[...] = hidq_ref[...].T

    def down(i, carry):
        col = pl.ds(pl.multiple_of(i * 256, 256), 256)
        accd_s[...] = nn(hidt_s[...], dbr_ref[:, col]) + nn(hidtq_s[...], dbrq_ref[:, col])
        put_rows(own_ref, send_ref, core, accd_s, per_down, pl.multiple_of(i * per_down, 16), (0,))
        return carry

    lax.fori_loop(0, width // 256, down, 0)
    base = (width // 256) * per_down
    n2t_s[...] = n2_ref[...].T
    n2tq_s[...] = n2q_ref[...].T
    steps = hidden // 512
    for which, (d, dq) in enumerate(((dg_ref, dgq_ref), (du_ref, duq_ref))):

        def gate(i, carry, d=d, dq=dq, start=base + which * steps * 2 * per):
            col = pl.ds(pl.multiple_of(i * 512, 512), 512)
            acc_s[...] = nn(n2t_s[...], d[:, col]) + nn(n2tq_s[...], dq[:, col])
            put_rows(own_ref, send_ref, core, acc_s, per, pl.multiple_of(start + i * 2 * per, 16), (0, 256))
            return carry

        lax.fori_loop(0, steps, gate, 0)
    base = base + 2 * steps * 2 * per
    acc_s[...] = nn(mixt_ref[...], datt_ref[:, 0:512]) + nn(mixtq_ref[...], dattq_ref[:, 0:512])
    put_rows(own_ref, send_ref, core, acc_s, per, base, (0, 256))
    base = base + 2 * per
    acc_s[:, 0:256] = nn(mixt_ref[...], datt_ref[:, 512:768]) + nn(mixtq_ref[...], dattq_ref[:, 512:768])
    accp_s[...] = nn(n3_ref[...].T, dpj_ref[...]) + nn(n3q_ref[...].T, dpjq_ref[...])

    def proj_rows(rows):
        return jnp.concatenate([accp_s[rows, :], jnp.zeros((per, LANE), F32)], axis=1)

    put_rows(own_ref, send_ref, core, acc_s, per, base, (0,), extra=proj_rows)


def ff_grads(core, pairs, count):
    flat = [a for pair in pairs for a in pair]
    tokens, width = pairs[0][0].shape
    qtokens = pairs[0][1].shape[0]
    hidden = pairs[1][0].shape[1]
    per, per_down = width // (2 * count), hidden // (2 * count)
    rows = (width // 256) * per_down + (2 * (hidden // 256) + 4) * per
    out = shape_of((count, rows, 256), BF16)
    return call(
        ff_grad_kernel,
        "ff_weight_grads",
        [out, out],
        [core, *flat],
        [SM] + [VM] * len(flat),
        [
            pltpu.VMEM((width, tokens), BF16),
            pltpu.VMEM((width, qtokens), BF16),
            pltpu.VMEM((hidden, tokens), BF16),
            pltpu.VMEM((hidden, qtokens), BF16),
            pltpu.VMEM((width, 512), F32),
            pltpu.VMEM((hidden, 256), F32),
            pltpu.VMEM((width, LANE), F32),
        ],
        48,
        2 * (tokens + 256) * (width * width + 3 * width * hidden),
        24 << 20,
    )


def qkv_grad_kernel(core_ref, n1_ref, n1q_ref, d_ref, dq_ref, own_ref, send_ref, n1t_s, n1tq_s, acc_s):
    core = core_ref[0]
    width = n1_ref.shape[1]
    count = own_ref.shape[0]
    per = width // (2 * count)
    n1t_s[...] = n1_ref[...].T
    n1tq_s[...] = n1q_ref[...].T
    steps = (3 * width) // 512

    def body(i, carry):
        col = pl.ds(pl.multiple_of(i * 512, 512), 512)
        acc_s[...] = nn(n1t_s[...], d_ref[:, col]) + nn(n1tq_s[...], dq_ref[:, col])
        put_rows(own_ref, send_ref, core, acc_s, per, pl.multiple_of(i * 2 * per, 16), (0, 256))
        return carry

    lax.fori_loop(0, steps, body, 0)
    lo = steps * 512
    acc_s[:, 0:256] = nn(n1t_s[...], d_ref[:, lo:lo + 256]) + nn(n1tq_s[...], dq_ref[:, lo:lo + 256])
    put_rows(own_ref, send_ref, core, acc_s, per, steps * 2 * per, (0,), pad=8)


def qkv_grads(core, n1, n1q, d, dq, count):
    tokens, width = n1.shape
    per = width // (2 * count)
    rows = 9 * per + 8
    out = shape_of((count, rows, 256), BF16)
    return call(
        qkv_grad_kernel,
        "qkv_weight_grads",
        [out, out],
        [core, n1, n1q, d, dq],
        [SM] + [VM] * 4,
        [
            pltpu.VMEM((width, tokens), BF16),
            pltpu.VMEM((width, n1q.shape[0]), BF16),
            pltpu.VMEM((width, 512), F32),
        ],
        32,
        2 * (tokens + 256) * 3 * width * width,
        10 << 20,
    )


def shard_sum(own, send, n_dp, n_grp):
    dp, grp = lax.axis_index("dp"), lax.axis_index("grp")
    nz = n_dp // 2
    z, x, y = dp // 2, dp % 2, grp // 2
    rows, cols = own.shape[1:]
    got = lax.ppermute(send, "grp", [(i, i ^ 1) for i in range(n_grp)])
    own5, got5 = own.reshape(nz, 2, 2, rows, cols), got.reshape(nz, 2, 2, rows, cols)

    def piece(xx, yy):
        take = lambda a: lax.dynamic_slice(a, (0, xx, yy, 0, 0), (nz, 1, 1, rows, cols)).reshape(nz, rows, cols)
        return take(own5).astype(F32) + take(got5).astype(F32)

    across = [(d * n_grp + g, (d ^ 1) * n_grp + (g ^ 2)) for d in range(n_dp) for g in range(n_grp)]
    from_xy = lax.ppermute(piece(1 - x, 1 - y).astype(BF16), ("dp", "grp"), across)
    from_x = lax.ppermute(piece(1 - x, y).astype(BF16), "dp", [(d, d ^ 1) for d in range(n_dp)])
    from_y = lax.ppermute(piece(x, 1 - y).astype(BF16), "grp", [(g, g ^ 2) for g in range(n_grp)])
    line = piece(x, y) + from_x.astype(F32) + from_y.astype(F32) + from_xy.astype(F32)
    total = lax.dynamic_slice(line, (z, 0, 0), (1, rows, cols))[0]
    for k in range(1, nz):
        part = lax.dynamic_slice(line, ((z + k) % nz, 0, 0), (1, rows, cols))[0].astype(BF16)
        total = total + lax.ppermute(part, "dp", [(d, (d + 2 * k) % n_dp) for d in range(n_dp)]).astype(F32)
    return total


def unfold(rows, per, width):
    parts = width // 256
    return jnp.transpose(rows.reshape(parts, per, 256), (1, 0, 2)).reshape(per, width)


def on_device(
    n_dp, n_grp, doc_tokens, doc_lengths, query_tokens, query_lengths, candidates, labels, gain_attn, w_query, w_key,
    w_value, w_out, bias_table, gain_ffn, w_gate, w_up, w_down, gain_final, w_proj,
):
    doc_rows, doc_len, width = doc_tokens.shape
    query_rows, query_len = query_tokens.shape[:2]
    hidden = w_gate.shape[1]
    bucket_total, heads = bias_table.shape
    devices = n_dp * n_grp
    axes = ("dp", "grp")
    dp, grp = lax.axis_index("dp"), lax.axis_index("grp")
    x_doc = doc_tokens.reshape(doc_len, width)
    x_qry = query_tokens.reshape(query_rows * query_len, width)
    gains = jnp.stack([gain_attn, gain_ffn, gain_final]).astype(F32)
    weights = (w_query, w_key, w_value, w_out, w_gate, w_up, w_down, w_proj)
    hot = jnp.asarray(strip_onehot(), BF16)
    ints = jnp.concatenate([candidates.T, labels[None, :], query_lengths[None, :]]).astype(BF16)
    ints = jnp.pad(ints, ((0, PACK_INT - ints.shape[0]), (0, LANE - query_rows)))

    (q_q, q_k, q_v, q_e, q_il, q_mixt, q_mid, q_n1, q_n2, q_hid, q_a, q_b, q_out, q_n3, q_proj, packed, base) = forward(
        x_qry, query_lengths, gains, (bias_table, hot, ints), weights, False, heads
    )
    got = lax.all_to_all(jnp.broadcast_to(packed[None], (n_dp, *packed.shape)), "dp", 0, 0, tiled=True)
    (d_q, d_k, d_v, d_e, d_il, d_mixt, d_mid, d_n1, d_n2, d_hid, d_a, d_b, d_out, d_n3, d_proj, emb) = forward(
        x_doc, doc_lengths, gains, base, weights, True, heads
    )
    sums, lse = scores(got, emb, doc_lengths, query_len)
    sums = lax.all_to_all(sums, "dp", 0, 0, tiled=True)
    demb_doc, demb_part, loss_group = retrieval_back(
        got, sums, emb, lse, doc_lengths, dp.astype(jnp.int32).reshape(1), query_len
    )
    demb_qry = lax.all_to_all(demb_part, "dp", 0, 0, tiled=True)
    back = (w_proj, w_down, w_gate, w_up, w_out)
    d_dpj, d_dbr, d_dg, d_du, d_datt, d_dmid, d_dmix, d_dmixt, d_dgain = chain(
        demb_doc, d_proj, d_out, d_mid, d_a, d_b, gains, *back, "doc_ff_back"
    )
    q_dpj, q_dbr, q_dg, q_du, q_datt, q_dmid, q_dmix, q_dmixt, q_dgain = chain(
        demb_qry, q_proj, q_out, q_mid, q_a, q_b, gains, *back, "query_ff_back"
    )
    fast = (n_dp, n_grp) == (8, 4)
    core = (grp % 2).astype(jnp.int32).reshape(1)
    if fast:
        ff_own, ff_send = ff_grads(
            core,
            (
                (d_n2, q_n2), (d_hid, q_hid), (d_n3, q_n3), (d_mixt, q_mixt), (d_dg, q_dg), (d_du, q_du),
                (d_dbr, q_dbr), (d_dpj, q_dpj), (d_datt, q_datt),
            ),
            devices // 2,
        )
        ff = shard_sum(ff_own, ff_send, n_dp, n_grp)
    d_dqkv, d_diag, d_far = attention_back(d_q, d_k, d_v, d_e, d_il, d_mixt, d_dmix, d_dmixt, "doc_attention_back")
    q_dqkv, q_diag, q_far = attention_back(q_q, q_k, q_v, q_e, q_il, q_mixt, q_dmix, q_dmixt, "query_attention_back")
    if fast:
        qkv_own, qkv_send = qkv_grads(core, d_n1, q_n1, d_dqkv, q_dqkv, devices // 2)
        qkv = shard_sum(qkv_own, qkv_send, n_dp, n_grp)
    doc_grad, d_dgain1 = input_back(d_dqkv, d_dmid, x_doc, gains, w_query, w_key, w_value, "doc_input_back")
    query_grad, q_dgain1 = input_back(q_dqkv, q_dmid, x_qry, gains, w_query, w_key, w_value, "query_input_back")

    far = jnp.sum((d_far + q_far).reshape(heads, 2, -1), axis=-1)
    dtable = lax.dot_general(
        hot.astype(F32),
        (d_diag + q_diag).reshape(heads, -1),
        (((1,), (1,)), ((), ())),
        precision=highest,
        preferred_element_type=F32,
    )
    half = bucket_total // 2
    dtable = dtable.at[half - 1].add(far[:, 0]).at[bucket_total - 1].add(far[:, 1])
    dgains = jnp.concatenate([d_dgain1 + q_dgain1, d_dgain + q_dgain])
    part_loss = loss_group[0, 0] / n_dp
    query_total = query_rows * devices
    per = width // devices

    small = jnp.transpose(dgains.reshape(3, devices, per), (1, 0, 2)).reshape(devices, 3 * per)
    same = jnp.concatenate([dtable.reshape(-1), part_loss.reshape(1)])
    small = jnp.concatenate([small, jnp.broadcast_to(same[None], (devices, same.shape[0]))], axis=1)
    cut = -(-small.shape[1] // LANE) * LANE
    small = jnp.pad(small, ((0, 0), (0, cut - small.shape[1])))
    small = jnp.sum(lax.all_to_all(small, axes, 0, 0, tiled=True), axis=0)
    shard_gains = small[: 3 * per].reshape(3, per)
    table_grad = small[3 * per:3 * per + bucket_total * heads].reshape(bucket_total, heads)
    loss = small[3 * per + bucket_total * heads] / query_total

    if fast:
        per_down = hidden // devices
        at = (width // 256) * per_down
        shard_down = unfold(ff[:at], per_down, width)
        shard_gate = unfold(ff[at:at + (hidden // 256) * per], per, hidden)
        at = at + (hidden // 256) * per
        shard_up = unfold(ff[at:at + (hidden // 256) * per], per, hidden)
        at = at + (hidden // 256) * per
        shard_out = unfold(ff[at:at + 3 * per], per, width)
        shard_proj = ff[at + 3 * per:at + 4 * per, : w_proj.shape[1]]
        shard_query, shard_key, shard_value = (unfold(qkv[i * 3 * per:(i + 1) * 3 * per], per, width) for i in range(3))
    else:

        def grad(left, right):
            product = tn(jnp.concatenate(left), jnp.concatenate(right))
            return lax.psum_scatter(product, axes, scatter_dimension=0, tiled=True)

        n1s = (d_n1, q_n1)
        shard_query, shard_key, shard_value = (
            grad(n1s, (d_dqkv[:, i * width:(i + 1) * width], q_dqkv[:, i * width:(i + 1) * width])) for i in range(3)
        )
        shard_out = grad((d_mixt.T, q_mixt.T), (d_datt, q_datt))
        shard_gate = grad((d_n2, q_n2), (d_dg, q_dg))
        shard_up = grad((d_n2, q_n2), (d_du, q_du))
        shard_down = grad((d_hid, q_hid), (d_dbr, q_dbr))
        shard_proj = grad((d_n3, q_n3), (d_dpj, q_dpj))
    return (
        loss,
        doc_grad.reshape(doc_rows, doc_len, width),
        query_grad.reshape(query_rows, query_len, width),
        shard_gains[0],
        shard_query,
        shard_key,
        shard_value,
        shard_out,
        table_grad,
        shard_gains[1],
        shard_gate,
        shard_up,
        shard_down,
        shard_gains[2],
        shard_proj,
    )


def solution(mesh):
    both = ("dp", "grp")
    rows3, rows2, rows1 = P(both, None, None), P(both, None), P(both)
    in_specs = (rows3, rows2, rows3, rows1, rows2, rows1) + (P(),) * 12
    out_specs = (
        P(), rows3, rows3, rows1, rows2, rows2, rows2, rows2, P(), rows1, rows2, rows2, rows2, rows1, rows2,
    )
    body = functools.partial(on_device, mesh.shape["dp"], mesh.shape["grp"])
    return jax.shard_map(body, mesh=mesh, in_specs=in_specs, out_specs=out_specs, check_vma=False)
```

time: 1160 us -> 325 us (0.28)
  waiting for transfers between devices: 744 us -> 105 us
  matrix products: 160 us -> 0.32 us
  Pallas kernels: 0 us -> 120 us
  blocking collectives: 84.9 us -> 0 us
  local copies, waits for them, and re-layouts: 101 us -> 35 us
  starting transfers between devices: 4.32 us -> 40.2 us
  other arithmetic: 38.8 us -> 20.2 us
  between operations: 17.3 us -> 3.38 us
    reduce_scatter x8 -> x0, waiting for transfers between devices: 739 us -> none  [the longest x1 121 us: on_device(): lax.psum_scatter(grad_gate, ('dp', 'grp'), scatter_dimension=0, tiled=True)]
    dot_general x51 -> x1, matrix products: 160 us -> 0.32 us  [on_device(): lax.dot_general(hot.astype(F32), (d_diag + q_diag).reshape(heads, -1), ((...]
    pallas_call x0 -> x12, Pallas kernels: none -> 120 us  [call(): pl.pallas_call(kernel, name=name, out_shape=outs, in_specs=specs, out_spe...]
    all_to_all x1 -> x4, waiting for transfers between devices: 5.16 us -> 75.6 us  [the longest x1 68.9 us: on_device(): small = jnp.sum(lax.all_to_all(small, axes, 0, 0, tiled=True), axis=0)]
    psum x1 -> x0, blocking collectives: 40.7 us -> none  [on_device(): loss_total, table_grad = lax.psum((local_loss, dtable), ('dp', 'grp'))]
    transpose x3 -> x1, local copies, waits for them, and re-layouts: 34.4 us -> 0.07 us  [on_device(): jnp.transpose(dgains.reshape(3, devices, per), (1, 0, 2))]
    all_gather x1 -> x0, blocking collectives: 32.3 us -> none  [on_device(): gathered = lax.all_gather(probe_embedded, 'dp', axis=0, tiled=True)]
    ppermute x0 -> x14, waiting for transfers between devices: none -> 28.9 us  [the longest x6 28.9 us: shard_sum(): lax.ppermute(part, 'dp', [(d, (d + 2 * k) % n_dp) for d in range(n_dp)])]
  transfers between devices with their start and end apart: 10 -> 18, of which waited for: 9 -> 5; matrix products, arithmetic and copies ran while one was open for 12% -> 8% of each run, Pallas kernels for 0% -> 23%
where the time goes in v1:
time: 325 us; the launch traced here: 324 us
  Pallas kernels  120 us (37%)
  waiting for transfers between devices  105 us (32%)
  starting transfers between devices  40.2 us (12%)
  local copies, waits for them, and re-layouts  35 us (11%)
  other arithmetic  20.2 us (6%)
  between operations  3.38 us (1%)
    pallas_call x12, Pallas kernels, call(): pl.pallas_call(kernel, name=name, out_shape=outs, in_specs=specs, out_spe...  120 us
    all_to_all x1, waiting for transfers between devices, on_device(): small = jnp.sum(lax.all_to_all(small, axes, 0, 0, tiled=True), axis=0)  68.9 us
    ppermute x6, waiting for transfers between devices, shard_sum(): lax.ppermute(part, 'dp', [(d, (d + 2 * k) % n_dp) for d in range(n_dp)])  28.9 us
    unnamed x127, local copies, waits for them, and re-layouts  21.2 us
    ppermute x6, starting transfers between devices, shard_sum(): lax.ppermute(part, 'dp', [(d, (d + 2 * k) % n_dp) for d in range(n_dp)])  9.52 us
    convert_element_type x2, other arithmetic, shard_sum(): piece(1 - x, y).astype(BF16)  8.7 us
    all_to_all x1, starting transfers between devices, on_device(): lax.all_to_all(jnp.broadcast_to(packed[None], (n_dp, *packed.shape)), 'dp...  7.25 us
    all_to_all x1, waiting for transfers between devices, on_device(): sums = lax.all_to_all(sums, 'dp', 0, 0, tiled=True)  6.69 us
  transfers between devices with their start and end apart: 18, of which 5 were waited for; matrix products, arithmetic and copies ran while one was open for 8% of the time, Pallas kernels for 23%

profile of v1, /device:TPU:0, one launch (start us, length us, event | category | flops | bytes accessed | tf_op | source)
XLA Modules:
  0.0 324.1 jit_solution(6513720723411842858)
XLA Ops:
  3.5 1.4 copy.152.tab_ref
  6.8 10.6 %query_forward.1 = (bf16[64,768]{1,0:T(8,128)(2,1)}, bf16[64,768]{1,0:T(8,128)(2,1)}, bf16[64,768]{1,0:T(8,128)(2,1)}, bf16[12,64,64]{2,1,0:T(8,128)(2,1)}, f32[...) custom-call(bf16[64,768]{1,0:T(8,128)(2,1)} %bitcast.151, ...), custom_call_target="tpu_custom_call" | custom-call | flops 931135488 | bytes 31457280 | tf_op jit(solution)/shard_map/query_forward/pallas_call | solution.py:67
  17.4 1.5 broadcast_in_dim.22
  18.9 7.3 %all-to-all-start = ((bf16[8,112,128]{2,1,0:T(8,128)(2,1)}), bf16[8,112,128]{2,1,0:T(8,128)(2,1)S(1)}, u32[]{:S(2)}, u32[]{:S(2)}) async-start(bf16[8,112,128]{2,1,0:T(8,128)(2,1)} %broadcast_in_dim.22), calls=%async_computation | async-start | bytes 458752 | tf_op jit(solution)/shard_map/all_to_all | solution.py:813
  26.1 30.7 %doc_forward.1 = (bf16[512,768]{1,0:T(8,128)(2,1)}, bf16[512,768]{1,0:T(8,128)(2,1)}, bf16[512,768]{1,0:T(8,128)(2,1)}, bf16[12,512,512]{2,1,0:T(8,128)(2,1)}, f...) custom-call(bf16[512,768]{1,0:T(8,128)(2,1)} %bitcast.149, ...), custom_call_target="tpu_custom_call" | custom-call | flops 8153726976 | bytes 31457280 | tf_op jit(solution)/shard_map/doc_forward/pallas_call | solution.py:67
  56.8 0.9 copy-done.25
  57.7 1.9 block_sums.1
  59.7 6.0 %all-to-all-start.1 = ((f32[8,8,128]{2,1,0:T(8,128)}), f32[8,8,128]{2,1,0:T(8,128)S(1)}, u32[]{:S(2)}, u32[]{:S(2)}) async-start(f32[8,8,128]{2,1,0:T(8,128)} %get-tuple-element.118), calls=%async_computation.1 | async-start | bytes 65536 | tf_op jit(solution)/shard_map/all_to_all | solution.py:818
  65.6 6.7 %all-to-all-done.1.sums_ref = f32[8,8,128]{2,1,0:T(8,128)S(1)} async-done(((f32[8,8,128]{2,1,0:T(8,128)}), f32[8,8,128]{2,1,0:T(8,128)S(1)}, u32[]{:S(2)}, u32[]{:S(2)}) %all-to-all-start.1) | async-done | bytes 32800 | tf_op jit(solution)/shard_map/all_to_all | solution.py:818
  72.3 0.9 copy-done.26
  73.2 2.3 retrieval_back.1
  75.5 0.7 copy-done.47
  76.2 3.6 %all-to-all-start.2 = ((f32[8,64,128]{2,1,0:T(8,128)}), f32[8,64,128]{2,1,0:T(8,128)S(1)}, u32[]{:S(2)}, u32[]{:S(2)}) async-start(f32[8,64,128]{2,1,0:T(8,128)} %get-tuple-element.137), calls=%async_computation.2 | async-start | bytes 524288 | tf_op jit(solution)/shard_map/all_to_all | solution.py:822
  79.8 18.9 %doc_ff_back.1 = (bf16[512,128]{1,0:T(8,128)(2,1)}, bf16[512,768]{1,0:T(8,128)(2,1)}, bf16[512,2048]{1,0:T(8,128)(2,1)}, bf16[512,2048]{1,0:T(8,128)(2,1)}, bf16...) custom-call(f32[512,128]{1,0:T(8,128)} %copy-done.47, ...), custom_call_target="tpu_custom_call" | custom-call | flops 5536481280 | bytes 31457280 | tf_op jit(solution)/shard_map/doc_ff_back/pallas_call | solution.py:67
  98.7 0.7 copy-done.55
  99.5 11.2 %query_ff_back.1 = (bf16[64,128]{1,0:T(8,128)(2,1)}, bf16[64,768]{1,0:T(8,128)(2,1)}, bf16[64,2048]{1,0:T(8,128)(2,1)}, bf16[64,2048]{1,0:T(8,128)(2,1)}, bf16[6...) custom-call(f32[8,64,128]{2,1,0:T(8,128)} %copy-done.55, ...), custom_call_target="tpu_custom_call" | custom-call | flops 692060160 | bytes 31457280 | tf_op jit(solution)/shard_map/query_ff_back/pallas_call | solution.py:67
  110.8 1.1 copy-done.39
  111.9 1.1 copy-done.40
  113.0 0.9 copy-done.44
  113.9 0.9 copy-done.45
  114.7 0.7 copy-done.46
  115.5 19.3 %ff_weight_grads.1 = (bf16[16,672,256]{2,1,0:T(8,128)(2,1)}, bf16[16,672,256]{2,1,0:T(8,128)(2,1)}) custom-call(s32[1]{0:T(128)} %bitcast.16.core_ref, bf16[512,768]{1,0:T(8,128)(2,1)S(1)} %copy-done.52, bf16[64,768]{1,0:T(8,128)(2,1)S(1)} %copy-done.42, bf16[512,2048]{1,0:T(8,128)(2,1)} %get-tuple-element.163.hid_ref, bf16[64,2048]{1,0:T(8,128)(2,1)S(1)} %copy-done.38, ...), custom_call_target="tpu_custom_call" | custom-call | flops 8153726976 | bytes 25165824 | tf_op jit(solution)/shard_map/ff_weight_grads/pallas_call | solution.py:67
  135.0 8.8 %doc_attention_back.1 = (bf16[512,2304]{1,0:T(8,128)(2,1)S(1)}, f32[12,8,512]{2,1,0:T(8,128)S(1)}, f32[12,16,128]{2,1,0:T(8,128)S(1)}) custom-call(bf16[512,768]{1,0:T(8,128)(2,1)S(1)} %copy-done.9, bf16[512,768]{1,0:T(8,128)(2,1)S(1)} %copy-done.10, bf16[512,768]{1,0:T(8,128)(2,1)S(1)} %copy-done.11, bf16[12,512,512]{2,1,0:T(8,128)(2,1)S(1)} %bitcast.146, ...), custom_call_target="tpu_custom_call" | custom-call | flops 2013265920 | bytes 16777216 | tf_op jit(solution)/shard_map/doc_attention_back/pallas_call | solution.py:67
  143.9 3.2 %query_attention_back.1 = (bf16[64,2304]{1,0:T(8,128)(2,1)S(1)}, f32[12,8,512]{2,1,0:T(8,128)S(1)}, f32[12,16,128]{2,1,0:T(8,128)S(1)}) custom-call(bf16[64,768]{1,0:T(8,128)(2,1)S(1)} %copy-done.31, bf16[64,768]{1,0:T(8,128)(2,1)S(1)} %copy-done.32, bf16[64,768]{1,0:T(8,128)(2,1)S(1)} %copy-done.33, bf16[12,64,64]{2,1,0:T(8,128)(2,1)S(1)} %copy-done.22, ...), custom_call_target="tpu_custom_call" | custom-call | flops 31457280 | bytes 16777216 | tf_op jit(solution)/shard_map/query_attention_back/pallas_call | solution.py:67
  147.2 5.7 %qkv_weight_grads.1 = (bf16[16,224,256]{2,1,0:T(8,128)(2,1)S(1)}, bf16[16,224,256]{2,1,0:T(8,128)(2,1)}) custom-call(s32[1]{0:T(128)} %bitcast.16.core_ref, bf16[512,768]{1,0:T(8,128)(2,1)S(1)} %copy-done.51, bf16[64,768]{1,0:T(8,128)(2,1)S(1)} %copy-done.41, bf16[512,2304]{1,0:T(8,128)(2,1)S(1)} %get-tuple-element.128.dqkv_ref.d_ref, ...), custom_call_target="tpu_custom_call" | custom-call | flops 2717908992 | bytes 10485760 | tf_op jit(solution)/shard_map/qkv_weight_grads/pallas_call | solution.py:67
  152.9 1.2 copy-done.5
  154.7 1.7 copy-done.4
  156.4 1.4 copy-done.7
  157.8 1.1 copy-done.8
  158.9 4.9 %doc_input_back.1 = (f32[512,768]{1,0:T(8,128)}, f32[1,768]{1,0:T(1,128)S(1)}) custom-call(bf16[512,2304]{1,0:T(8,128)(2,1)S(1)} %copy-done.4, f32[512,768]{1,0:T(8,128)S(1)} %copy-done.7, bf16[512,768]{1,0:T(8,128)(2,1)S(1)} %bitcast.150, f32[3,768]{1,0:T(4,128)S(1)} %copy-done.16, bf16[768,768]{1,0:T(8,128)(2,1)S(1)} %copy-done, ...), custom_call_target="tpu_custom_call" | custom-call | flops 1811939328 | bytes 8388608 | tf_op jit(solution)/shard_map/doc_input_back/pallas_call | solution.py:67
  163.9 0.7 add_reduce_fusion
  164.6 1.4 copy.154
  166.0 0.7 bitcast_reduce_fusion
  167.2 1.3 copy.157
  168.6 1.3 copy.184
  169.9 1.0 add.205
  171.1 0.7 add.204
  171.9 0.9 copy-done.15
  172.8 1.0 copy-done.18
  173.7 0.9 copy-done.19
  174.6 2.9 query_input_back.1
  178.0 2.6 fusion.9
  180.6 1.9 collective-permute-start.1
  182.6 6.1 %fusion.2 = (bf16[4,672,256]{2,1,0:T(8,128)(2,1)}, bf16[4,672,256]{2,1,0:T(8,128)(2,1)}, bf16[4,672,256]{2,1,0:T(8,128)(2,1)S(1)}) fusion(bf16[4,2,2,672,256]{4,3,2,1,0:T(8,128)(2,1)} %bitcast.34, s32[]{:T(128)S(6)} %select_n.101, s32[]{:T(128)S(6)} %select_n.100, bf16[4,2,2,672,256]{4,3,2,1,0:T(8,128)(2,1)} %bitcast.154, s32[]{:T(128)S(6)} %select_n.98, ...), kind=kLoop, calls=%fused_computation.6 | loop fusion | flops 8257536 | bytes 12386320 | tf_op jit(solution)/shard_map/convert_element_type | solution.py:776
  188.7 1.5 collective-permute-start.9
  190.3 1.8 collective-permute-start.10
  192.9 1.5 collective-permute-start.2
  194.4 2.8 collective-permute-start.3
  197.9 3.7 %all-to-all-start.3 = ((f32[32,1,512]{2,1,0:T(1,128)}), f32[32,1,512]{2,1,0:T(1,128)S(1)}, u32[]{:S(2)}, u32[]{:S(2)}) async-start(f32[32,1,512]{2,1,0:T(1,128)} %all_to_all.18), calls=%async_computation.3 | async-start | bytes 131072 | tf_op jit(solution)/shard_map/all_to_all | solution.py:870
  201.6 68.9 %all-to-all-done.3 = f32[32,1,512]{2,1,0:T(1,128)S(1)} async-done(((f32[32,1,512]{2,1,0:T(1,128)}), f32[32,1,512]{2,1,0:T(1,128)S(1)}, u32[]{:S(2)}, u32[]{:S(2)}) %all-to-all-start.3) | async-done | bytes 65568 | tf_op jit(solution)/shard_map/all_to_all | solution.py:870
  273.3 1.9 fusion.6
  275.3 1.8 collective-permute-start.4
  277.1 2.1 collective-permute-start.6
  279.1 0.9 collective-permute-start.5
  280.0 3.4 %fusion.1 = f32[4,672,256]{2,1,0:T(8,128)S(1)} fusion(bf16[4,672,256]{2,1,0:T(8,128)(2,1)} %collective-permute-done.10, bf16[4,672,256]{2,1,0:T(8,128)(2,1)} %collective-permute-done.9, bf16[4,672,256]{2,1,0:T(8,128)(2,1)S(1)} %collective-permute-done.8, bf16[4,2,2,672,256]{4,3,2,1,0:T(8,128)(2,1)} %bitcast.34, s32[]{:T(128)S(6)} %select_n.98, ...), kind=kLoop, calls=%fused_computation.2 | loop fusion | flops 6193152 | bytes 9633800 | tf_op jit(solution)/shard_map/add | solution.py:778
  283.5 1.5 collective-permute-start.11
  285.0 2.3 collective-permute-start.13
  287.4 0.9 collective-permute-start.12
  288.3 8.9 %collective-permute-done.5 = bf16[224,256]{1,0:T(8,128)(2,1)S(1)} collective-permute-done((bf16[224,256]{1,0:T(8,128)(2,1)S(1)}, bf16[224,256]{1,0:T(8,128)(2,1)S(1)}, u32[]{:S(2)}, u32[]{:S(2)}) %collective-permute-start.5) | collective-permute-done | bytes 114720 | tf_op jit(solution)/shard_map/ppermute | solution.py:782
  299.2 4.6 %collective-permute-done.13 = bf16[672,256]{1,0:T(8,128)(2,1)S(1)} collective-permute-done((bf16[672,256]{1,0:T(8,128)(2,1)S(1)}, bf16[672,256]{1,0:T(8,128)(2,1)S(1)}, u32[]{:S(2)}, u32[]{:S(2)}) %collective-permute-start.13) | collective-permute-done | bytes 344096 | tf_op jit(solution)/shard_map/ppermute | solution.py:782
  303.7 15.5 %collective-permute-done.12 = bf16[672,256]{1,0:T(8,128)(2,1)S(1)} collective-permute-done((bf16[672,256]{1,0:T(8,128)(2,1)S(1)}, bf16[672,256]{1,0:T(8,128)(2,1)S(1)}, u32[]{:S(2)}, u32[]{:S(2)}) %collective-permute-start.12) | collective-permute-done | bytes 344096 | tf_op jit(solution)/shard_map/ppermute | solution.py:782
  320.0 0.7 copy.205
  321.6 0.7 copy.208
  322.3 0.7 copy.204
  (168 shorter events, 14.1 us)
Async XLA Ops:
  18.9 37.9 %all-to-all-start = ((bf16[8,112,128]{2,1,0:T(8,128)(2,1)}), bf16[8,112,128]{2,1,0:T(8,128)(2,1)S(1)}, u32[]{:S(2)}, u32[]{:S(2)}) async-start(bf16[8,112,128]{2,1,0:T(8,128)(2,1)} %broadcast_in_dim.22), calls=%async_computation | async-start | bytes 458752 | tf_op jit(solution)/shard_map/all_to_all | solution.py:813
  26.1 30.7 %copy-start.37 = (s32[1,4]{1,0:T(1,128)S(1)}, s32[1,4]{1,0:T(1,128)}, u32[]{:S(2)}) copy-start(s32[1,4]{1,0:T(1,128)} %lens_ref.7) | copy-start | bytes 52
  59.7 12.7 %all-to-all-start.1 = ((f32[8,8,128]{2,1,0:T(8,128)}), f32[8,8,128]{2,1,0:T(8,128)S(1)}, u32[]{:S(2)}, u32[]{:S(2)}) async-start(f32[8,8,128]{2,1,0:T(8,128)} %get-tuple-element.118), calls=%async_computation.1 | async-start | bytes 65536 | tf_op jit(solution)/shard_map/all_to_all | solution.py:818
  76.2 22.5 %all-to-all-start.2 = ((f32[8,64,128]{2,1,0:T(8,128)}), f32[8,64,128]{2,1,0:T(8,128)S(1)}, u32[]{:S(2)}, u32[]{:S(2)}) async-start(f32[8,64,128]{2,1,0:T(8,128)} %get-tuple-element.137), calls=%async_computation.2 | async-start | bytes 524288 | tf_op jit(solution)/shard_map/all_to_all | solution.py:822
  99.4 11.3 %copy-start.12 = (bf16[768,512]{1,0:T(8,128)(2,1)S(1)}, bf16[768,512]{1,0:T(8,128)(2,1)}, u32[]{:S(2)}) copy-start(bf16[768,512]{1,0:T(8,128)(2,1)} %get-tuple-element.115.mixt_ref) | copy-start | bytes 2359300
  99.4 11.3 %copy-start.23 = (bf16[768,64]{1,0:T(8,128)(2,1)S(1)}, bf16[768,64]{1,0:T(8,128)(2,1)}, u32[]{:S(2)}) copy-start(bf16[768,64]{1,0:T(8,128)(2,1)} %get-tuple-element.136.mixt_ref.mixtq_ref) | copy-start | bytes 294916
  99.4 11.3 %copy-start.38 = (bf16[64,2048]{1,0:T(8,128)(2,1)S(1)}, bf16[64,2048]{1,0:T(8,128)(2,1)}, u32[]{:S(2)}) copy-start(bf16[64,2048]{1,0:T(8,128)(2,1)} %get-tuple-element.164.hidq_ref) | copy-start | bytes 786436
  99.4 11.3 %copy-start.42 = (bf16[64,768]{1,0:T(8,128)(2,1)S(1)}, bf16[64,768]{1,0:T(8,128)(2,1)}, u32[]{:S(2)}) copy-start(bf16[64,768]{1,0:T(8,128)(2,1)} %get-tuple-element.162.n2q_ref) | copy-start | bytes 294916
  99.4 11.3 %copy-start.43 = (bf16[64,768]{1,0:T(8,128)(2,1)S(1)}, bf16[64,768]{1,0:T(8,128)(2,1)}, u32[]{:S(2)}) copy-start(bf16[64,768]{1,0:T(8,128)(2,1)} %get-tuple-element.166.n3q_ref) | copy-start | bytes 294916
  99.4 11.3 %copy-start.48 = (bf16[512,768]{1,0:T(8,128)(2,1)S(1)}, bf16[512,768]{1,0:T(8,128)(2,1)}, u32[]{:S(2)}) copy-start(bf16[512,768]{1,0:T(8,128)(2,1)} %get-tuple-element.171.dbr_ref) | copy-start | bytes 2359300
  99.4 11.3 %copy-start.49 = (bf16[512,768]{1,0:T(8,128)(2,1)S(1)}, bf16[512,768]{1,0:T(8,128)(2,1)}, u32[]{:S(2)}) copy-start(bf16[512,768]{1,0:T(8,128)(2,1)} %get-tuple-element.175.datt_ref) | copy-start | bytes 2359300
  99.4 11.3 %copy-start.50 = (bf16[512,128]{1,0:T(8,128)(2,1)S(1)}, bf16[512,128]{1,0:T(8,128)(2,1)}, u32[]{:S(2)}) copy-start(bf16[512,128]{1,0:T(8,128)(2,1)} %get-tuple-element.173.dpj_ref) | copy-start | bytes 393220
  99.5 11.3 %copy-start.52 = (bf16[512,768]{1,0:T(8,128)(2,1)S(1)}, bf16[512,768]{1,0:T(8,128)(2,1)}, u32[]{:S(2)}) copy-start(bf16[512,768]{1,0:T(8,128)(2,1)} %get-tuple-element.161.n2_ref) | copy-start | bytes 2359300
  99.5 11.3 %copy-start.53 = (bf16[512,768]{1,0:T(8,128)(2,1)S(1)}, bf16[512,768]{1,0:T(8,128)(2,1)}, u32[]{:S(2)}) copy-start(bf16[512,768]{1,0:T(8,128)(2,1)} %get-tuple-element.165.n3_ref) | copy-start | bytes 2359300
  110.7 24.2 %slice-start = ((s8[6291456]{0:T(1024)(128)(4,1)}), s8[4194304]{0:T(1024)(128)(4,1)S(1)}, s32[]{:S(2)}) async-start(s8[6291456]{0:T(1024)(128)(4,1)} %bitcast.145), calls=%async_computation.4 | async-start | bytes 8388608
  115.5 19.4 %slice-start.1 = ((s8[6291456]{0:T(1024)(128)(4,1)}), s8[2097152]{0:T(1024)(128)(4,1)S(1)}, s32[]{:S(2)}) async-start(s8[6291456]{0:T(1024)(128)(4,1)} %bitcast.145), calls=%async_computation.5 | async-start | bytes 4194304
  115.5 19.4 %copy-start.9 = (bf16[512,768]{1,0:T(8,128)(2,1)S(1)}, bf16[512,768]{1,0:T(8,128)(2,1)}, u32[]{:S(2)}) copy-start(bf16[512,768]{1,0:T(8,128)(2,1)} %get-tuple-element.110.q_ref) | copy-start | bytes 2359300
  115.5 19.4 %copy-start.10 = (bf16[512,768]{1,0:T(8,128)(2,1)S(1)}, bf16[512,768]{1,0:T(8,128)(2,1)}, u32[]{:S(2)}) copy-start(bf16[512,768]{1,0:T(8,128)(2,1)} %get-tuple-element.111.k_ref) | copy-start | bytes 2359300
  115.5 19.4 %copy-start.11 = (bf16[512,768]{1,0:T(8,128)(2,1)S(1)}, bf16[512,768]{1,0:T(8,128)(2,1)}, u32[]{:S(2)}) copy-start(bf16[512,768]{1,0:T(8,128)(2,1)} %get-tuple-element.112.v_ref) | copy-start | bytes 2359300
  115.5 19.4 %copy-start.13 = (bf16[512,768]{1,0:T(8,128)(2,1)S(1)}, bf16[512,768]{1,0:T(8,128)(2,1)}, u32[]{:S(2)}) copy-start(bf16[512,768]{1,0:T(8,128)(2,1)} %get-tuple-element.126.dmix_ref) | copy-start | bytes 2359300
  115.5 19.4 %copy-start.14 = (bf16[768,512]{1,0:T(8,128)(2,1)S(1)}, bf16[768,512]{1,0:T(8,128)(2,1)}, u32[]{:S(2)}) copy-start(bf16[768,512]{1,0:T(8,128)(2,1)} %get-tuple-element.127.dmixt_ref) | copy-start | bytes 2359300
  115.5 19.4 %copy-start.35 = (f32[12,1,512]{2,1,0:T(1,128)S(1)}, f32[12,1,512]{2,1,0:T(1,128)}, u32[]{:S(2)}) copy-start(f32[12,1,512]{2,1,0:T(1,128)} %get-tuple-element.114.il_ref) | copy-start | bytes 73732
  134.8 47.7 %collective-permute-start.7 = (bf16[16,672,256]{2,1,0:T(8,128)(2,1)}, bf16[16,672,256]{2,1,0:T(8,128)(2,1)}, u32[]{:S(2)}, u32[]{:S(2)}) collective-permute-start(bf16[16,672,256]{2,1,0:T(8,128)(2,1)} %get-tuple-element.178), channel_id=1, source_target_pairs={{0,1},{1,0},{2,3},{3,2},{4,5},{5,4},{6,7},{7,6},{8,9},{9,8},{10,11... | collective-permute-start | bytes 16515080 | tf_op jit(solution)/shard_map/ppermute | solution.py:767
  134.9 8.9 %copy-start.22 = (bf16[12,64,64]{2,1,0:T(8,128)(2,1)S(1)}, bf16[12,64,64]{2,1,0:T(8,128)(2,1)}, u32[]{:S(2)}) copy-start(bf16[12,64,64]{2,1,0:T(8,128)(2,1)} %get-tuple-element.134.e_ref) | copy-start | bytes 294916
  134.9 8.9 %copy-start.24 = (bf16[768,64]{1,0:T(8,128)(2,1)S(1)}, bf16[768,64]{1,0:T(8,128)(2,1)}, u32[]{:S(2)}) copy-start(bf16[768,64]{1,0:T(8,128)(2,1)} %get-tuple-element.144.dmixt_ref) | copy-start | bytes 294916
  134.9 8.9 %copy-start.31 = (bf16[64,768]{1,0:T(8,128)(2,1)S(1)}, bf16[64,768]{1,0:T(8,128)(2,1)}, u32[]{:S(2)}) copy-start(bf16[64,768]{1,0:T(8,128)(2,1)} %get-tuple-element.131.q_ref) | copy-start | bytes 294916
  134.9 8.9 %copy-start.32 = (bf16[64,768]{1,0:T(8,128)(2,1)S(1)}, bf16[64,768]{1,0:T(8,128)(2,1)}, u32[]{:S(2)}) copy-start(bf16[64,768]{1,0:T(8,128)(2,1)} %get-tuple-element.132.k_ref) | copy-start | bytes 294916
  135.0 8.9 %copy-start.33 = (bf16[64,768]{1,0:T(8,128)(2,1)S(1)}, bf16[64,768]{1,0:T(8,128)(2,1)}, u32[]{:S(2)}) copy-start(bf16[64,768]{1,0:T(8,128)(2,1)} %get-tuple-element.133.v_ref) | copy-start | bytes 294916
  135.0 8.9 %copy-start.34 = (bf16[64,768]{1,0:T(8,128)(2,1)S(1)}, bf16[64,768]{1,0:T(8,128)(2,1)}, u32[]{:S(2)}) copy-start(bf16[64,768]{1,0:T(8,128)(2,1)} %get-tuple-element.143.dmix_ref) | copy-start | bytes 294916
  135.0 8.9 %copy-start.36 = (f32[12,1,64]{2,1,0:T(1,128)S(1)}, f32[12,1,64]{2,1,0:T(1,128)}, u32[]{:S(2)}) copy-start(f32[12,1,64]{2,1,0:T(1,128)} %get-tuple-element.135.il_ref) | copy-start | bytes 9220
  135.0 12.2 %copy-start.41 = (bf16[64,768]{1,0:T(8,128)(2,1)S(1)}, bf16[64,768]{1,0:T(8,128)(2,1)}, u32[]{:S(2)}) copy-start(bf16[64,768]{1,0:T(8,128)(2,1)} %get-tuple-element.158.n1q_ref) | copy-start | bytes 294916
  135.0 12.2 %copy-start.51 = (bf16[512,768]{1,0:T(8,128)(2,1)S(1)}, bf16[512,768]{1,0:T(8,128)(2,1)}, u32[]{:S(2)}) copy-start(bf16[512,768]{1,0:T(8,128)(2,1)} %get-tuple-element.157.n1_ref) | copy-start | bytes 2359300
  143.8 9.1 %copy-start.3 = (bf16[512,2304]{1,0:T(8,128)(2,1)}, bf16[512,2304]{1,0:T(8,128)(2,1)S(1)}, u32[]{:S(2)}) copy-start(bf16[512,2304]{1,0:T(8,128)(2,1)S(1)} %get-tuple-element.128.dqkv_ref.d_ref) | copy-start | bytes 7077892
  143.8 9.1 %copy-start.20 = (f32[12,8,512]{2,1,0:T(8,128)}, f32[12,8,512]{2,1,0:T(8,128)S(1)}, u32[]{:S(2)}) copy-start(f32[12,8,512]{2,1,0:T(8,128)S(1)} %get-tuple-element.150) | copy-start | bytes 589828
  143.8 9.1 %copy-start.27 = (f32[12,16,128]{2,1,0:T(8,128)}, f32[12,16,128]{2,1,0:T(8,128)S(1)}, u32[]{:S(2)}) copy-start(f32[12,16,128]{2,1,0:T(8,128)S(1)} %get-tuple-element.152) | copy-start | bytes 294916
  147.1 5.8 %copy-start.17 = (bf16[64,2304]{1,0:T(8,128)(2,1)}, bf16[64,2304]{1,0:T(8,128)(2,1)S(1)}, u32[]{:S(2)}) copy-start(bf16[64,2304]{1,0:T(8,128)(2,1)S(1)} %get-tuple-element.145.dqkv_ref.dq_ref) | copy-start | bytes 884740
  147.1 5.8 %copy-start.21 = (f32[12,8,512]{2,1,0:T(8,128)}, f32[12,8,512]{2,1,0:T(8,128)S(1)}, u32[]{:S(2)}) copy-start(f32[12,8,512]{2,1,0:T(8,128)S(1)} %get-tuple-element.151) | copy-start | bytes 589828
  147.2 5.8 %copy-start.29 = (f32[12,16,128]{2,1,0:T(8,128)}, f32[12,16,128]{2,1,0:T(8,128)S(1)}, u32[]{:S(2)}) copy-start(f32[12,16,128]{2,1,0:T(8,128)S(1)} %get-tuple-element.153) | copy-start | bytes 294916
  147.2 7.5 %copy-start = (bf16[768,768]{1,0:T(8,128)(2,1)S(1)}, bf16[768,768]{1,0:T(8,128)(2,1)}, u32[]{:S(2)}) copy-start(bf16[768,768]{1,0:T(8,128)(2,1)} %wq.5) | copy-start | bytes 3538948
  147.2 7.5 %copy-start.1 = (bf16[768,768]{1,0:T(8,128)(2,1)S(1)}, bf16[768,768]{1,0:T(8,128)(2,1)}, u32[]{:S(2)}) copy-start(bf16[768,768]{1,0:T(8,128)(2,1)} %wk.5) | copy-start | bytes 3538948
  147.2 7.5 %copy-start.2 = (bf16[768,768]{1,0:T(8,128)(2,1)S(1)}, bf16[768,768]{1,0:T(8,128)(2,1)}, u32[]{:S(2)}) copy-start(bf16[768,768]{1,0:T(8,128)(2,1)} %wv.5) | copy-start | bytes 3538948
  147.2 7.5 %copy-start.16 = (f32[3,768]{1,0:T(4,128)S(1)}, f32[3,768]{1,0:T(4,128)}, u32[]{:S(2)}) copy-start(f32[3,768]{1,0:T(4,128)} %maximum_convert_fusion.gains_ref) | copy-start | bytes 27652
  154.2 23.8 %collective-permute-start = (bf16[16,224,256]{2,1,0:T(8,128)(2,1)}, bf16[16,224,256]{2,1,0:T(8,128)(2,1)}, u32[]{:S(2)}, u32[]{:S(2)}) collective-permute-start(bf16[16,224,256]{2,1,0:T(8,128)(2,1)} %get-tuple-element.160), channel_id=1, source_target_pairs={{0,1},{1,0},{2,3},{3,2},{4,5},{5,4},{6,7},{7,6},{8,9},{9,8},{10,11... | collective-permute-start | bytes 5505032 | tf_op jit(solution)/shard_map/ppermute | solution.py:767
  154.7 1.7 copy-start.4
  156.4 1.4 copy-start.7
  158.9 5.0 %copy-start.28 = (f32[12,16,128]{2,1,0:T(8,128)S(1)}, f32[12,16,128]{2,1,0:T(8,128)}, u32[]{:S(2)}) copy-start(f32[12,16,128]{2,1,0:T(8,128)} %copy-done.27) | copy-start | bytes 294916
  158.9 5.0 %copy-start.30 = (f32[12,16,128]{2,1,0:T(8,128)S(1)}, f32[12,16,128]{2,1,0:T(8,128)}, u32[]{:S(2)}) copy-start(f32[12,16,128]{2,1,0:T(8,128)} %copy-done.29) | copy-start | bytes 294916
  171.0 6.6 %copy-start.54 = (bf16[32,4096]{1,0:T(8,128)(2,1)S(1)}, bf16[32,4096]{1,0:T(8,128)(2,1)}, u32[]{:S(2)}) copy-start(bf16[32,4096]{1,0:T(8,128)(2,1)} %constant.150.clone.hot_ref) | copy-start | bytes 786436
  174.6 3.3 %copy-start.57 = (f32[12,1]{1,0:T(8,128)S(1)}, f32[12,1]{1,0:T(8,128)}, u32[]{:S(2)}) copy-start(f32[12,1]{1,0:T(8,128)} %copy.184) | copy-start | bytes 148
  174.6 3.4 %copy-start.6 = (bf16[16,224,256]{2,1,0:T(8,128)(2,1)S(1)}, bf16[16,224,256]{2,1,0:T(8,128)(2,1)}, u32[]{:S(2)}) copy-start(bf16[16,224,256]{2,1,0:T(8,128)(2,1)} %copy-done.5) | copy-start | bytes 5505028
  180.6 13.8 %collective-permute-start.1 = (bf16[4,224,256]{2,1,0:T(8,128)(2,1)}, bf16[4,224,256]{2,1,0:T(8,128)(2,1)}, u32[]{:S(2)}, u32[]{:S(2)}) collective-permute-start(bf16[4,224,256]{2,1,0:T(8,128)(2,1)} %get-tuple-element.242), channel_id=1, source_target_pairs={{0,4},{4,0},{8,12},{12,8},{16,20},{20,16},{24,28},{28,24},{1,5},{5... | collective-permute-start | bytes 1376264 | tf_op jit(solution)/shard_map/ppermute | solution.py:776
  182.5 9.9 %copy-start.56 = (f32[1,12]{0,1:T(8,128)S(1)}, f32[1,12]{0,1:T(8,128)}, u32[]{:S(2)}) copy-start(f32[1,12]{0,1:T(8,128)} %copy.157) | copy-start | bytes 148
  188.6 90.5 %collective-permute-start.8 = (bf16[4,672,256]{2,1,0:T(8,128)(2,1)}, bf16[4,672,256]{2,1,0:T(8,128)(2,1)S(1)}, u32[]{:S(2)}, u32[]{:S(2)}) collective-permute-start(bf16[4,672,256]{2,1,0:T(8,128)(2,1)} %get-tuple-element.239), channel_id=1, source_target_pairs={{0,4},{4,0},{8,12},{12,8},{16,20},{20,16},{24,28},{28,24},{1,5},{5... | collective-permute-start | bytes 4128776 | tf_op jit(solution)/shard_map/ppermute | solution.py:776
  188.7 91.3 %collective-permute-start.9 = (bf16[4,672,256]{2,1,0:T(8,128)(2,1)}, bf16[4,672,256]{2,1,0:T(8,128)(2,1)}, u32[]{:S(2)}, u32[]{:S(2)}) collective-permute-start(bf16[4,672,256]{2,1,0:T(8,128)(2,1)} %get-tuple-element.240), channel_id=1, source_target_pairs={{0,2},{1,3},{2,0},{3,1},{4,6},{5,7},{6,4},{7,5},{8,10},{9,11},{10,... | collective-permute-start | bytes 4128776 | tf_op jit(solution)/shard_map/ppermute | solution.py:777
  190.3 89.7 %collective-permute-start.10 = (bf16[4,672,256]{2,1,0:T(8,128)(2,1)S(1)}, bf16[4,672,256]{2,1,0:T(8,128)(2,1)}, u32[]{:S(2)}, u32[]{:S(2)}) collective-permute-start(bf16[4,672,256]{2,1,0:T(8,128)(2,1)S(1)} %get-tuple-element.241), channel_id=1, source_target_pairs={{0,6},{1,7},{2,4},{3,5},{4,2},{5,3},{6,0},{7,1},{8,14},{9,15},{10,... | collective-permute-start | bytes 4128776 | tf_op jit(solution)/shard_map/ppermute | solution.py:775
  192.9 80.4 %collective-permute-start.2 = (bf16[4,224,256]{2,1,0:T(8,128)(2,1)}, bf16[4,224,256]{2,1,0:T(8,128)(2,1)}, u32[]{:S(2)}, u32[]{:S(2)}) collective-permute-start(bf16[4,224,256]{2,1,0:T(8,128)(2,1)} %get-tuple-element.243), channel_id=1, source_target_pairs={{0,2},{1,3},{2,0},{3,1},{4,6},{5,7},{6,4},{7,5},{8,10},{9,11},{10,... | collective-permute-start | bytes 1376264 | tf_op jit(solution)/shard_map/ppermute | solution.py:777
  194.4 78.9 %collective-permute-start.3 = (bf16[4,224,256]{2,1,0:T(8,128)(2,1)S(1)}, bf16[4,224,256]{2,1,0:T(8,128)(2,1)}, u32[]{:S(2)}, u32[]{:S(2)}) collective-permute-start(bf16[4,224,256]{2,1,0:T(8,128)(2,1)S(1)} %get-tuple-element.244), channel_id=1, source_target_pairs={{0,6},{1,7},{2,4},{3,5},{4,2},{5,3},{6,0},{7,1},{8,14},{9,15},{10,... | collective-permute-start | bytes 1376264 | tf_op jit(solution)/shard_map/ppermute | solution.py:775
  197.9 72.7 %all-to-all-start.3 = ((f32[32,1,512]{2,1,0:T(1,128)}), f32[32,1,512]{2,1,0:T(1,128)S(1)}, u32[]{:S(2)}, u32[]{:S(2)}) async-start(f32[32,1,512]{2,1,0:T(1,128)} %all_to_all.18), calls=%async_computation.3 | async-start | bytes 131072 | tf_op jit(solution)/shard_map/all_to_all | solution.py:870
  275.3 12.1 %collective-permute-start.4 = (bf16[224,256]{1,0:T(8,128)(2,1)S(1)}, bf16[224,256]{1,0:T(8,128)(2,1)S(1)}, u32[]{:S(2)}, u32[]{:S(2)}) collective-permute-start(bf16[224,256]{1,0:T(8,128)(2,1)S(1)} %get-tuple-element.248), channel_id=1, source_target_pairs={{0,8},{4,12},{8,16},{12,20},{16,24},{20,28},{24,0},{28,4},{1,9},{5... | collective-permute-start | bytes 344072 | tf_op jit(solution)/shard_map/ppermute | solution.py:782
  277.1 11.3 %collective-permute-start.6 = (bf16[224,256]{1,0:T(8,128)(2,1)S(1)}, bf16[224,256]{1,0:T(8,128)(2,1)S(1)}, u32[]{:S(2)}, u32[]{:S(2)}) collective-permute-start(bf16[224,256]{1,0:T(8,128)(2,1)S(1)} %get-tuple-element.249), channel_id=1, source_target_pairs={{0,24},{4,28},{8,0},{12,4},{16,8},{20,12},{24,16},{28,20},{1,25},{... | collective-permute-start | bytes 344072 | tf_op jit(solution)/shard_map/ppermute | solution.py:782
  279.1 18.1 %collective-permute-start.5 = (bf16[224,256]{1,0:T(8,128)(2,1)S(1)}, bf16[224,256]{1,0:T(8,128)(2,1)S(1)}, u32[]{:S(2)}, u32[]{:S(2)}) collective-permute-start(bf16[224,256]{1,0:T(8,128)(2,1)S(1)} %get-tuple-element.250), channel_id=1, source_target_pairs={{0,16},{4,20},{8,24},{12,28},{16,0},{20,4},{24,8},{28,12},{1,17},{... | collective-permute-start | bytes 344072 | tf_op jit(solution)/shard_map/ppermute | solution.py:782
  283.5 15.7 %collective-permute-start.11 = (bf16[672,256]{1,0:T(8,128)(2,1)S(1)}, bf16[672,256]{1,0:T(8,128)(2,1)S(1)}, u32[]{:S(2)}, u32[]{:S(2)}) collective-permute-start(bf16[672,256]{1,0:T(8,128)(2,1)S(1)} %get-tuple-element.245), channel_id=1, source_target_pairs={{0,8},{4,12},{8,16},{12,20},{16,24},{20,28},{24,0},{28,4},{1,9},{5... | collective-permute-start | bytes 1032200 | tf_op jit(solution)/shard_map/ppermute | solution.py:782
  285.0 18.7 %collective-permute-start.13 = (bf16[672,256]{1,0:T(8,128)(2,1)S(1)}, bf16[672,256]{1,0:T(8,128)(2,1)S(1)}, u32[]{:S(2)}, u32[]{:S(2)}) collective-permute-start(bf16[672,256]{1,0:T(8,128)(2,1)S(1)} %get-tuple-element.246), channel_id=1, source_target_pairs={{0,24},{4,28},{8,0},{12,4},{16,8},{20,12},{24,16},{28,20},{1,25},{... | collective-permute-start | bytes 1032200 | tf_op jit(solution)/shard_map/ppermute | solution.py:782
  287.4 31.8 %collective-permute-start.12 = (bf16[672,256]{1,0:T(8,128)(2,1)S(1)}, bf16[672,256]{1,0:T(8,128)(2,1)S(1)}, u32[]{:S(2)}, u32[]{:S(2)}) collective-permute-start(bf16[672,256]{1,0:T(8,128)(2,1)S(1)} %get-tuple-element.247), channel_id=1, source_target_pairs={{0,16},{4,20},{8,24},{12,28},{16,0},{20,4},{24,8},{28,12},{1,17},{... | collective-permute-start | bytes 1032200 | tf_op jit(solution)/shard_map/ppermute | solution.py:782
  (14 other events, 13.1 us)
